TPU v7x, 32 devices: a whole 2x2x4 slice. The times are simulated.
32 devices in a mesh: dp: 8 (over y, x, core), seq: 4 (over z).
Axes of the slice: x: 2, y: 2, z: 4, core: 2. Of those that a mesh axis runs over, the one named last changes fastest.
Arguments:
- tokens: bfloat16 [8, 1024, 896], P('dp', 'seq'), may hold values from -6 to 6
- segments: int32 [8, 1024], P('dp', 'seq'), may hold values from 0 to 2, as said below
- cotangent: bfloat16 [8, 1024, 896], P('dp', 'seq'), may hold values from -6 to 6
- attn_gain: bfloat16 [896], P('seq'), may hold values from 0.5 to 1.5
- w_query: bfloat16 [896, 896], P('dp', 'seq'), may hold values from -0.1875 to 0.1875
- b_query: bfloat16 [896], P('seq'), may hold values from -3 to 3
- w_key: bfloat16 [896, 128], P('dp', 'seq'), may hold values from -0.1875 to 0.1875
- b_key: bfloat16 [128], P('seq'), may hold values from -3 to 3
- w_value: bfloat16 [896, 128], P('dp', 'seq'), may hold values from -0.1875 to 0.1875
- b_value: bfloat16 [128], P('seq'), may hold values from -3 to 3
- w_out: bfloat16 [896, 896], P('dp', 'seq'), may hold values from -0.75 to 0.75
- mlp_gain: bfloat16 [896], P('seq'), may hold values from 0.5 to 1.5
- w_gate: bfloat16 [896, 4864], P('dp', 'seq'), may hold values from -0.1875 to 0.1875
- w_up: bfloat16 [896, 4864], P('dp', 'seq'), may hold values from -0.1875 to 0.1875
- w_down: bfloat16 [4864, 896], P('seq', 'dp'), may hold values from -0.078125 to 0.078125
Outputs:
- output: bfloat16 [8, 1024, 896], P('dp', 'seq')
- input_grad: float32 [8, 1024, 896], P('dp', 'seq')
- grad_attn_gain: float32 [896], P('seq')
- grad_w_query: float32 [896, 896], P('dp', 'seq')
- grad_b_query: float32 [896], P('seq')
- grad_w_key: float32 [896, 128], P('dp', 'seq')
- grad_b_key: float32 [128], P('seq')
- grad_w_value: float32 [896, 128], P('dp', 'seq')
- grad_b_value: float32 [128], P('seq')
- grad_w_out: float32 [896, 896], P('dp', 'seq')
- grad_mlp_gain: float32 [896], P('seq')
- grad_w_gate: float32 [896, 4864], P('dp', 'seq')
- grad_w_up: float32 [896, 4864], P('dp', 'seq')
- grad_w_down: float32 [4864, 896], P('seq', 'dp')
Inputs may be any that keep to these rules, and one draw needn't show every extreme that they name: `segments`: in each sequence the numbers start at 0 and never fall; document 1 begins within the first 256 tokens and ends within the last 256.
All inputs are finite; a program needn't handle non-finite values.
Results may differ from a plain program's by a relative error of at most 0.02.
Values may be sent and summed in bfloat16 or wider, within the bound.
A program may use at most 192 MiB of HBM per device.

v0:
```python
import jax
import jax.numpy as jnp
from jax import lax
from jax.sharding import PartitionSpec as P

H = 14
KVH = 2
HD = 64


norm_eps = 1e-06
rope_base = 1000000.0


def contract(left_mat, right_mat, left_dim, right_dim):
    return lax.dot_general(
        left_mat,
        right_mat,
        (((left_dim,), (right_dim,)), ((), ())),
        preferred_element_type=jnp.float32,
    )


def angle_tables(positions, head_dim):
    half_dim = head_dim // 2
    frequency = rope_base ** (-2.0 * jnp.arange(half_dim, dtype=jnp.float32) / head_dim)
    angles = positions.astype(jnp.float32)[:, None] * frequency[None, :]
    return (jnp.cos(angles)[:, None, :], jnp.sin(angles)[:, None, :])


def rotate(heads_field, cosine, sine_table):
    half_dim = heads_field.shape[-1] // 2
    first_half = heads_field[..., :half_dim]
    second = heads_field[..., half_dim:]
    return jnp.concatenate(
        [first_half * cosine - second * sine_table, second * cosine + first_half * sine_table],
        axis=-1,
    )


def unrotate(grad_field, cosine, sine_table):
    half_dim = grad_field.shape[-1] // 2
    first_half = grad_field[..., :half_dim]
    second = grad_field[..., half_dim:]
    return jnp.concatenate(
        [first_half * cosine + second * sine_table, second * cosine - first_half * sine_table],
        axis=-1,
    )


def score_block(query_rot, key_all, query_seg, key_seg, query_pos, key_pos):
    scores = (
        jnp.einsum("qgjd,kgd->gjqk", query_rot, key_all, preferred_element_type=jnp.float32) * 0.125
    )
    allowed = (query_seg[:, None] == key_seg[None, :]) & (query_pos[:, None] >= key_pos[None, :])
    return jnp.where(allowed, scores, -1e30)


def on_device(
    tokens,
    segments,
    cotangent,
    attn_gain,
    w_query,
    b_query,
    w_key,
    b_key,
    w_value,
    b_value,
    w_out,
    mlp_gain,
    w_gate,
    w_up,
    w_down,
):
    seq_rows = tokens.shape[0]
    local_len = tokens.shape[1]
    model_width = tokens.shape[2]
    seq_count = lax.axis_size("seq")
    seq_place = lax.axis_index("seq")
    full_len = local_len * seq_count
    group_size = H // KVH
    row_count = seq_rows * local_len
    pieces = (
        lax.all_gather(w_query, "seq", axis=1, tiled=True),
        lax.all_gather(w_key, "seq", axis=1, tiled=True),
        lax.all_gather(w_value, "seq", axis=1, tiled=True),
        lax.all_gather(w_out, "seq", axis=1, tiled=True),
        lax.all_gather(attn_gain, "seq", axis=0, tiled=True),
        lax.all_gather(b_query, "seq", axis=0, tiled=True),
        lax.all_gather(b_key, "seq", axis=0, tiled=True),
        lax.all_gather(b_value, "seq", axis=0, tiled=True),
        lax.all_gather(mlp_gain, "seq", axis=0, tiled=True),
    )
    gate_part, up_part, down_part = (
        lax.all_gather(w_gate, "seq", axis=1, tiled=True),
        lax.all_gather(w_up, "seq", axis=1, tiled=True),
        lax.all_gather(w_down, "seq", axis=0, tiled=True),
    )
    mat_query, mat_key, mat_value, mat_out, mat_gate, mat_up, mat_down = (
        lax.all_gather(pieces[0], "dp", axis=0, tiled=True),
        lax.all_gather(pieces[1], "dp", axis=0, tiled=True),
        lax.all_gather(pieces[2], "dp", axis=0, tiled=True),
        lax.all_gather(pieces[3], "dp", axis=0, tiled=True),
        lax.all_gather(gate_part, "dp", axis=0, tiled=True),
        lax.all_gather(up_part, "dp", axis=0, tiled=True),
        lax.all_gather(down_part, "dp", axis=1, tiled=True),
    )
    gain_one = pieces[4].astype(jnp.float32)
    bias_query = pieces[5].astype(jnp.float32)
    bias_key = pieces[6].astype(jnp.float32)
    bias_value = pieces[7].astype(jnp.float32)
    gain_two = pieces[8].astype(jnp.float32)
    own_pos = seq_place * local_len + jnp.arange(local_len, dtype=jnp.int32)
    all_pos = jnp.arange(full_len, dtype=jnp.int32)
    cosine, sine_table = angle_tables(own_pos, HD)
    inputs = tokens.astype(jnp.float32).reshape(row_count, model_width)
    scale_one = lax.rsqrt(jnp.mean(inputs * inputs, axis=-1, keepdims=True) + norm_eps)
    normed = (inputs * scale_one * gain_one).astype(jnp.bfloat16)
    query_lin = jnp.dot(normed, mat_query, preferred_element_type=jnp.float32) + bias_query
    key_lin = jnp.dot(normed, mat_key, preferred_element_type=jnp.float32) + bias_key
    value_lin = jnp.dot(normed, mat_value, preferred_element_type=jnp.float32) + bias_value
    query_rot = rotate(query_lin.reshape(seq_rows, local_len, H, HD), cosine, sine_table).astype(
        jnp.bfloat16
    )
    query_rot = query_rot.reshape(seq_rows, local_len, KVH, group_size, HD)
    key_rot = rotate(key_lin.reshape(seq_rows, local_len, KVH, HD), cosine, sine_table).astype(
        jnp.bfloat16
    )
    value_loc = value_lin.astype(jnp.bfloat16).reshape(seq_rows, local_len, KVH, HD)
    seg_own = segments.astype(jnp.bfloat16)
    key_all, value_all, seg_all = (
        lax.all_gather(key_rot, "seq", axis=1, tiled=True),
        lax.all_gather(value_loc, "seq", axis=1, tiled=True),
        lax.all_gather(seg_own, "seq", axis=1, tiled=True),
    )
    member = 0
    masked = score_block(
        query_rot[member], key_all[member], seg_own[member], seg_all[member], own_pos, all_pos
    )
    highest = jnp.max(masked, axis=-1, keepdims=True)
    weights = jnp.exp(masked - highest)
    totals = jnp.sum(weights, axis=-1, keepdims=True)
    prob_low = (weights / totals).astype(jnp.bfloat16)
    lse_list = [highest + jnp.log(totals)]
    outs_list = [
        jnp.einsum(
            "gjqk,kgd->qgjd", prob_low, value_all[member], preferred_element_type=jnp.float32
        )
    ]
    mixed = jnp.stack(outs_list).astype(jnp.bfloat16).reshape(row_count, model_width)
    residual = inputs + jnp.dot(mixed, mat_out, preferred_element_type=jnp.float32)
    scale_two = lax.rsqrt(jnp.mean(residual * residual, axis=-1, keepdims=True) + norm_eps)
    normed_two = (residual * scale_two * gain_two).astype(jnp.bfloat16)
    gate_lin = jnp.dot(normed_two, mat_gate, preferred_element_type=jnp.float32)
    up_lin = jnp.dot(normed_two, mat_up, preferred_element_type=jnp.float32)
    silu_gate = gate_lin / (1.0 + jnp.exp(-gate_lin))
    hidden = (silu_gate * up_lin).astype(jnp.bfloat16)
    branch_sum = jnp.dot(hidden, mat_down, preferred_element_type=jnp.float32)
    result = residual + branch_sum
    output = result.astype(jnp.bfloat16).reshape(seq_rows, local_len, model_width)
    d_result = cotangent.reshape(row_count, model_width)
    grad_down = contract(hidden, d_result, 0, 0)
    d_hidden = contract(d_result, mat_down, 1, 1)
    sigmoid_gate = 1.0 / (1.0 + jnp.exp(-gate_lin))
    d_gate = (
        d_hidden * up_lin * (sigmoid_gate + gate_lin * sigmoid_gate * (1.0 - sigmoid_gate))
    ).astype(jnp.bfloat16)
    d_up = (d_hidden * silu_gate).astype(jnp.bfloat16)
    grad_gate = contract(normed_two, d_gate, 0, 0)
    grad_up = contract(normed_two, d_up, 0, 0)
    d_norm_part = contract(d_gate, mat_gate, 1, 1) + contract(d_up, mat_up, 1, 1)
    grad_gain_two = jnp.sum(d_norm_part * residual * scale_two, axis=0)
    d_scaled_two = d_norm_part * gain_two
    d_residual = (
        d_result.astype(jnp.float32)
        + scale_two * d_scaled_two
        - residual * scale_two**3 * jnp.mean(d_scaled_two * residual, axis=-1, keepdims=True)
    )
    d_attn = d_residual.astype(jnp.bfloat16)
    grad_out = contract(mixed, d_attn, 0, 0)
    d_mixed = (
        contract(d_attn, mat_out, 1, 1)
        .astype(jnp.bfloat16)
        .reshape(seq_rows, local_len, KVH, group_size, HD)
    )
    member = 0
    masked = score_block(
        query_rot[member], key_all[member], seg_own[member], seg_all[member], own_pos, all_pos
    )
    prob_full = jnp.exp(masked - lse_list[member])
    prob_low = prob_full.astype(jnp.bfloat16)
    d_probs = jnp.einsum(
        "qgjd,kgd->gjqk", d_mixed[member], value_all[member], preferred_element_type=jnp.float32
    )
    dv_list = [
        jnp.einsum("gjqk,qgjd->kgd", prob_low, d_mixed[member], preferred_element_type=jnp.float32)
    ]
    d_scores = (
        prob_full * (d_probs - jnp.sum(d_probs * prob_full, axis=-1, keepdims=True))
    ).astype(jnp.bfloat16)
    dq_list = [
        jnp.einsum("gjqk,kgd->qgjd", d_scores, key_all[member], preferred_element_type=jnp.float32)
        * 0.125
    ]
    dk_list = [
        jnp.einsum(
            "gjqk,qgjd->kgd", d_scores, query_rot[member], preferred_element_type=jnp.float32
        )
        * 0.125
    ]
    d_key_full = jnp.stack(dk_list)
    d_value_full = jnp.stack(dv_list)
    d_key_loc, d_value_loc = (
        lax.psum_scatter(d_key_full, "seq", scatter_dimension=1, tiled=True),
        lax.psum_scatter(d_value_full, "seq", scatter_dimension=1, tiled=True),
    )
    d_query_rot = jnp.stack(dq_list).reshape(seq_rows, local_len, H, HD)
    d_query_lin = (
        unrotate(d_query_rot, cosine, sine_table)
        .astype(jnp.bfloat16)
        .reshape(row_count, model_width)
    )
    d_key_lin = (
        unrotate(d_key_loc, cosine, sine_table).astype(jnp.bfloat16).reshape(row_count, KVH * HD)
    )
    d_value_lin = d_value_loc.astype(jnp.bfloat16).reshape(row_count, KVH * HD)
    grad_query = contract(normed, d_query_lin, 0, 0)
    grad_key = contract(normed, d_key_lin, 0, 0)
    grad_value = contract(normed, d_value_lin, 0, 0)
    grad_bias_query = jnp.sum(d_query_lin, axis=0, dtype=jnp.float32)
    grad_bias_key = jnp.sum(d_key_lin, axis=0, dtype=jnp.float32)
    grad_bias_value = jnp.sum(d_value_lin, axis=0, dtype=jnp.float32)
    d_normed = (
        contract(d_query_lin, mat_query, 1, 1)
        + contract(d_key_lin, mat_key, 1, 1)
        + contract(d_value_lin, mat_value, 1, 1)
    )
    grad_gain_one = jnp.sum(d_normed * inputs * scale_one, axis=0)
    d_scaled = d_normed * gain_one
    d_inputs = (
        d_residual
        + scale_one * d_scaled
        - inputs * scale_one**3 * jnp.mean(d_scaled * inputs, axis=-1, keepdims=True)
    )
    dp_sums = (
        lax.psum_scatter(
            grad_query.astype(jnp.bfloat16), "dp", scatter_dimension=0, tiled=True
        ).astype(jnp.float32),
        lax.psum_scatter(
            grad_key.astype(jnp.bfloat16), "dp", scatter_dimension=0, tiled=True
        ).astype(jnp.float32),
        lax.psum_scatter(
            grad_value.astype(jnp.bfloat16), "dp", scatter_dimension=0, tiled=True
        ).astype(jnp.float32),
        lax.psum_scatter(
            grad_out.astype(jnp.bfloat16), "dp", scatter_dimension=0, tiled=True
        ).astype(jnp.float32),
        lax.psum_scatter(
            grad_gate.astype(jnp.bfloat16), "dp", scatter_dimension=0, tiled=True
        ).astype(jnp.float32),
        lax.psum_scatter(
            grad_up.astype(jnp.bfloat16), "dp", scatter_dimension=0, tiled=True
        ).astype(jnp.float32),
        lax.psum_scatter(
            grad_down.astype(jnp.bfloat16), "dp", scatter_dimension=1, tiled=True
        ).astype(jnp.float32),
    )
    attn_shards = (
        lax.psum_scatter(
            dp_sums[0].astype(jnp.bfloat16), "seq", scatter_dimension=1, tiled=True
        ).astype(jnp.float32),
        lax.psum_scatter(
            dp_sums[1].astype(jnp.bfloat16), "seq", scatter_dimension=1, tiled=True
        ).astype(jnp.float32),
        lax.psum_scatter(
            dp_sums[2].astype(jnp.bfloat16), "seq", scatter_dimension=1, tiled=True
        ).astype(jnp.float32),
        lax.psum_scatter(
            dp_sums[3].astype(jnp.bfloat16), "seq", scatter_dimension=1, tiled=True
        ).astype(jnp.float32),
    )
    mlp_shards = (
        lax.psum_scatter(
            dp_sums[4].astype(jnp.bfloat16), "seq", scatter_dimension=1, tiled=True
        ).astype(jnp.float32),
        lax.psum_scatter(
            dp_sums[5].astype(jnp.bfloat16), "seq", scatter_dimension=1, tiled=True
        ).astype(jnp.float32),
        lax.psum_scatter(
            dp_sums[6].astype(jnp.bfloat16), "seq", scatter_dimension=0, tiled=True
        ).astype(jnp.float32),
    )
    small_sums = lax.psum(
        (grad_gain_one, grad_bias_query, grad_bias_key, grad_bias_value, grad_gain_two),
        ("dp", "seq"),
    )

    def own_piece(vector):
        piece_len = vector.shape[0] // seq_count
        return lax.dynamic_slice_in_dim(vector, seq_place * piece_len, piece_len)

    input_grad = d_inputs.reshape(seq_rows, local_len, model_width)
    return (
        output,
        input_grad,
        own_piece(small_sums[0]),
        attn_shards[0],
        own_piece(small_sums[1]),
        attn_shards[1],
        own_piece(small_sums[2]),
        attn_shards[2],
        own_piece(small_sums[3]),
        attn_shards[3],
        own_piece(small_sums[4]),
        mlp_shards[0],
        mlp_shards[1],
        mlp_shards[2],
    )


def solution(mesh):
    return jax.shard_map(
        on_device,
        mesh=mesh,
        in_specs=(
            P("dp", "seq", None),
            P("dp", "seq"),
            P("dp", "seq", None),
            P("seq"),
            P("dp", "seq"),
            P("seq"),
            P("dp", "seq"),
            P("seq"),
            P("dp", "seq"),
            P("seq"),
            P("dp", "seq"),
            P("seq"),
            P("dp", "seq"),
            P("dp", "seq"),
            P("seq", "dp"),
        ),
        out_specs=(
            P("dp", "seq", None),
            P("dp", "seq", None),
            P("seq"),
            P("dp", "seq"),
            P("seq"),
            P("dp", "seq"),
            P("seq"),
            P("dp", "seq"),
            P("seq"),
            P("dp", "seq"),
            P("seq"),
            P("dp", "seq"),
            P("dp", "seq"),
            P("seq", "dp"),
        ),
        check_vma=False,
    )
```

profile of v0, /device:TPU:0, one launch (start us, length us, event | category | flops | bytes accessed | tf_op | source)
XLA Modules:
  0.0 992.2 jit_solution(12507651608595244472)
XLA Ops:
  10.4 15.9 %all_gather.76 = bf16[112,896]{0,1:T(8,128)(2,1)S(1)} all-gather(bf16[112,224]{0,1:T(8,128)(2,1)S(1)} %copy.71), channel_id=1, replica_groups=mesh['dp'=8,'seq'=4] {'seq'}, dimensions={1}, use_global_device_ids=true | all-gather | bytes 250880 | tf_op jit(solution)/shard_map/all_gather | solution.py:85
  28.1 16.4 %all_gather.79 = bf16[112,896]{0,1:T(8,128)(2,1)S(1)} all-gather(bf16[112,224]{0,1:T(8,128)(2,1)S(1)} %copy.75), channel_id=1, replica_groups=mesh['dp'=8,'seq'=4] {'seq'}, dimensions={1}, use_global_device_ids=true | all-gather | bytes 250880 | tf_op jit(solution)/shard_map/all_gather | solution.py:88
  50.6 26.5 %all-gather.22.cloned.1.call-done = bf16[4,1216,112]{1,2,0:T(8,128)(2,1)} async-done(((bf16[1,1216,112]{1,2,0:T(8,128)(2,1)}), bf16[4,1216,112]{1,2,0:T(8,128)(2,1)}) %all-gather.22.cloned.1.call-update) | async-done | bytes 1089552 | tf_op jit(solution)/shard_map/all_gather | solution.py:96
  80.9 26.8 %all-gather.26.cloned.1.call-done = bf16[4,1216,112]{1,2,0:T(8,128)(2,1)} async-done(((bf16[1,1216,112]{1,2,0:T(8,128)(2,1)}), bf16[4,1216,112]{1,2,0:T(8,128)(2,1)}) %all-gather.26.cloned.1.call-update) | async-done | bytes 1089552 | tf_op jit(solution)/shard_map/all_gather | solution.py:98
  125.5 13.1 %all_gather.72 = bf16[112,128]{0,1:T(8,128)(2,1)S(1)} all-gather(bf16[112,32]{0,1:T(8,128)(2,1)S(1)} %copy-done.29), channel_id=1, replica_groups=mesh['dp'=8,'seq'=4] {'seq'}, dimensions={1}, use_global_device_ids=true | all-gather | bytes 35840 | tf_op jit(solution)/shard_map/all_gather | solution.py:86
  138.8 13.1 %all_gather.67 = bf16[112,128]{0,1:T(8,128)(2,1)S(1)} all-gather(bf16[112,32]{0,1:T(8,128)(2,1)S(1)} %copy-done.30), channel_id=1, replica_groups=mesh['dp'=8,'seq'=4] {'seq'}, dimensions={1}, use_global_device_ids=true | all-gather | bytes 35840 | tf_op jit(solution)/shard_map/all_gather | solution.py:87
  179.8 13.9 %all_gather.70 = bf16[1,1024,2,64]{1,3,2,0:T(8,128)(2,1)S(1)} all-gather(bf16[1,256,2,64]{1,3,2,0:T(8,128)(2,1)S(1)} %bitcast.212), channel_id=1, replica_groups=mesh['dp'=8,'seq'=4] {'seq'}, dimensions={1}, use_global_device_ids=true | all-gather | bytes 327680 | tf_op jit(solution)/shard_map/all_gather | solution.py:134
  194.4 14.7 %all_gather.75 = bf16[1,1024,2,64]{1,3,2,0:T(8,128)(2,1)S(1)} all-gather(bf16[1,256,2,64]{1,3,2,0:T(8,128)(2,1)S(1)} %pad_maximum_fusion.3), channel_id=1, replica_groups=mesh['dp'=8,'seq'=4] {'seq'}, dimensions={1}, use_global_device_ids=true | all-gather | bytes 327680 | tf_op jit(solution)/shard_map/all_gather | solution.py:133
  246.8 32.0 %all-gather.16.cloned.1.call-done = bf16[896,4864]{1,0:T(8,128)(2,1)} async-done(((bf16[112,4864]{1,0:T(8,128)(2,1)}), bf16[896,4864]{1,0:T(8,128)(2,1)}) %all-gather.16.cloned.1.call-update) | async-done | bytes 8716304 | tf_op jit(solution)/shard_map/all_gather | solution.py:105
  286.6 49.8 %all-gather.20.cloned.1.call-done = bf16[4864,896]{0,1:T(8,128)(2,1)} async-done(((bf16[4864,112]{0,1:T(8,128)(2,1)}), bf16[4864,896]{0,1:T(8,128)(2,1)}) %all-gather.20.cloned.1.call-update) | async-done | bytes 8716304 | tf_op jit(solution)/shard_map/all_gather | solution.py:107
  336.5 10.5 %multiply_convert_fusion = (bf16[256,4864]{1,0:T(8,128)(2,1)S(1)}, bf16[256,4864]{1,0:T(8,128)(2,1)S(1)}, bf16[256,4864]{1,0:T(8,128)(2,1)}) fusion(f32[256,4864]{1,0:T(8,128)} %fusion.57, f32[256,4864]{1,0:T(8,128)} %fusion.58, bf16[4864,896]{0,1:T(8,128)(2,1)} %all-gather.20.cloned.1.call-done, bf16[1,256,896]{2,1,0:T(8,128)(2,1)S(1)} %copy-done.11), kind=kOutput, calls=%fused_computation.17 | convolution fusion | flops 2250047488 | bytes 26607616 | tf_op jit(solution)/shard_map/dot_general | solution.py:16
  379.5 10.8 %fusion.2 = bf16[2,7,256,1024]{2,3,1,0:T(8,128)(2,1)S(1)} fusion(f32[2,1024,256,7]{2,1,3,0:T(8,128)} %get-tuple-element.113, f32[2,7,256,1024]{2,3,1,0:T(8,128)} %get-tuple-element.108, f32[2,7,256]{2,1,0:T(8,128)} %get-tuple-element.112, f32[2,7,256]{2,1,0:T(8,128)S(1)} %log_add_fusion), kind=kLoop, calls=%fused_computation.4 | loop fusion | flops 14680064 | bytes 36728832 | tf_op jit(solution)/shard_map/convert_element_type | solution.py:201
  403.4 20.4 %reduce-scatter.31.cloned.1.call-done = f32[1,256,2,64]{1,3,2,0:T(8,128)} async-done(((f32[1,1024,2,64]{1,3,2,0:T(8,128)}), f32[1,256,2,64]{1,3,2,0:T(8,128)}) %reduce-scatter.31.cloned.1.call-update) | async-done | bytes 131088 | tf_op jit(solution)/shard_map/reduce_scatter | solution.py:215
  460.7 32.9 %reduce-scatter.37.cloned.1.call-done = bf16[112,128]{1,0:T(8,128)(2,1)} async-done(((bf16[896,128]{1,0:T(8,128)(2,1)}), bf16[112,128]{1,0:T(8,128)(2,1)}) %reduce-scatter.37.cloned.1.call-update) | async-done | bytes 28688 | tf_op jit(solution)/shard_map/reduce_scatter | solution.py:250
  495.1 40.7 %reduce-scatter.41.cloned.1.call-done = bf16[112,896]{1,0:T(8,128)(2,1)} async-done(((bf16[896,896]{1,0:T(8,128)(2,1)}), bf16[112,896]{1,0:T(8,128)(2,1)}) %reduce-scatter.41.cloned.1.call-update) | async-done | bytes 200720 | tf_op jit(solution)/shard_map/reduce_scatter | solution.py:256
  537.6 40.6 %reduce-scatter.35.cloned.1.call-done = bf16[112,896]{1,0:T(8,128)(2,1)} async-done(((bf16[896,896]{1,0:T(8,128)(2,1)}), bf16[112,896]{1,0:T(8,128)(2,1)}) %reduce-scatter.35.cloned.1.call-update) | async-done | bytes 200720 | tf_op jit(solution)/shard_map/reduce_scatter | solution.py:247
  580.1 74.5 %reduce-scatter.47.cloned.1.call-done = bf16[4864,112]{0,1:T(8,128)(2,1)} async-done(((bf16[4864,896]{0,1:T(8,128)(2,1)}), bf16[4864,112]{0,1:T(8,128)(2,1)}) %reduce-scatter.47.cloned.1.call-update) | async-done | bytes 1089552 | tf_op jit(solution)/shard_map/reduce_scatter | solution.py:265
  657.1 73.9 %reduce-scatter.45.cloned.1.call-done = bf16[112,4864]{1,0:T(8,128)(2,1)} async-done(((bf16[896,4864]{1,0:T(8,128)(2,1)}), bf16[112,4864]{1,0:T(8,128)(2,1)}) %reduce-scatter.45.cloned.1.call-update) | async-done | bytes 1089552 | tf_op jit(solution)/shard_map/reduce_scatter | solution.py:262
  733.8 73.6 %reduce-scatter.43.cloned.1.call-done = bf16[112,4864]{1,0:T(8,128)(2,1)} async-done(((bf16[896,4864]{1,0:T(8,128)(2,1)}), bf16[112,4864]{1,0:T(8,128)(2,1)}) %reduce-scatter.43.cloned.1.call-update) | async-done | bytes 1089552 | tf_op jit(solution)/shard_map/reduce_scatter | solution.py:259
  823.0 39.6 %all-reduce.5 = (f32[896]{0:T(1024)S(1)}, f32[896]{0:T(1024)S(1)}, f32[128]{0:T(128)S(1)}, f32[128]{0:T(128)S(1)}, f32[896]{0:T(1024)S(1)}) all-reduce(f32[896]{0:T(1024)S(1)} %get-tuple-element.72, f32[896]{0:T(1024)S(1)} %reduce_sum.113, f32[128]{0:T(128)S(1)} %reduce_sum.115, ...), channel_id=1, replica_groups=mesh['dp'=8,'seq'=4] {'dp','seq'}, use_global_device_ids=true, to_apply=%region_10.11 | all-reduce | flops 2944 | bytes 23552 | tf_op jit(solution)/shard_map/psum | solution.py:294
  871.5 18.1 %reduce-scatter.49.cloned.1.call-done = bf16[224,112]{1,0:T(8,128)(2,1)} async-done(((bf16[896,112]{1,0:T(8,128)(2,1)}), bf16[224,112]{1,0:T(8,128)(2,1)}) %reduce-scatter.49.cloned.1.call-update) | async-done | bytes 50192
  891.1 29.3 %reduce-scatter.61.cloned.1.call-done = bf16[1216,112]{1,0:T(8,128)(2,1)} async-done(((bf16[4864,112]{1,0:T(8,128)(2,1)}), bf16[1216,112]{1,0:T(8,128)(2,1)}) %reduce-scatter.61.cloned.1.call-update) | async-done | bytes 272400
  922.4 29.4 %reduce-scatter.59.cloned.1.call-done = bf16[1216,112]{1,0:T(8,128)(2,1)} async-done(((bf16[4864,112]{1,0:T(8,128)(2,1)}), bf16[1216,112]{1,0:T(8,128)(2,1)}) %reduce-scatter.59.cloned.1.call-update) | async-done | bytes 272400
  953.8 29.2 %reduce-scatter.57.cloned.1.call-done = bf16[1216,112]{1,0:T(8,128)(2,1)} async-done(((bf16[4864,112]{1,0:T(8,128)(2,1)}), bf16[1216,112]{1,0:T(8,128)(2,1)}) %reduce-scatter.57.cloned.1.call-update) | async-done | bytes 272400
  (254 shorter events, 229.7 us)
Async XLA Ops:
  7.2 39.8 %all-gather.24.cloned.1.call-start = ((), (), s32[]{:S(2)}) async-start(), calls=%async_computation.31 | async-start | bytes 1433600 | tf_op jit(solution)/shard_map/all_gather | solution.py:97
  7.9 69.2 %all-gather.22.cloned.1.call-start = ((), (), s32[]{:S(2)}) async-start(), calls=%async_computation.30 | async-start | bytes 1433600 | tf_op jit(solution)/shard_map/all_gather | solution.py:96
  8.7 99.1 %all-gather.26.cloned.1.call-start = ((), (), s32[]{:S(2)}) async-start(), calls=%async_computation.32 | async-start | bytes 1433600 | tf_op jit(solution)/shard_map/all_gather | solution.py:98
  9.4 199.9 %all-gather.12.cloned.1.call-start = ((), (), s32[]{:S(2)}) async-start(), calls=%async_computation.16 | async-start | bytes 1806336 | tf_op jit(solution)/shard_map/all_gather | solution.py:101
  27.1 208.6 %all-gather.14.cloned.1.call-start = ((), (), s32[]{:S(2)}) async-start(), calls=%async_computation.17 | async-start | bytes 1806336 | tf_op jit(solution)/shard_map/all_gather | solution.py:104
  45.3 193.6 %all-gather.18.cloned.1.call-start = ((), (), s32[]{:S(2)}) async-start(), calls=%async_computation.19 | async-start | bytes 9805824 | tf_op jit(solution)/shard_map/all_gather | solution.py:106
  50.6 228.2 %all-gather.16.cloned.1.call-start = ((), (), s32[]{:S(2)}) async-start(), calls=%async_computation.18 | async-start | bytes 9805824 | tf_op jit(solution)/shard_map/all_gather | solution.py:105
  80.8 255.6 %all-gather.20.cloned.1.call-start = ((), (), s32[]{:S(2)}) async-start(), calls=%async_computation.20 | async-start | bytes 9805824 | tf_op jit(solution)/shard_map/all_gather | solution.py:107
  111.3 289.9 %reduce-scatter.33.cloned.1.call-start = ((), (), s32[]{:S(2)}) async-start(), calls=%async_computation.22 | async-start | bytes 655360 | tf_op jit(solution)/shard_map/reduce_scatter | solution.py:216
  379.4 44.4 %reduce-scatter.31.cloned.1.call-start = ((), (), s32[]{:S(2)}) async-start(), calls=%async_computation.21 | async-start | bytes 655360 | tf_op jit(solution)/shard_map/reduce_scatter | solution.py:215
  396.3 62.8 %reduce-scatter.39.cloned.1.call-start = ((), (), s32[]{:S(2)}) async-start(), calls=%async_computation.25 | async-start | bytes 258048 | tf_op jit(solution)/shard_map/reduce_scatter | solution.py:253
  403.4 90.2 %reduce-scatter.37.cloned.1.call-start = ((), (), s32[]{:S(2)}) async-start(), calls=%async_computation.24 | async-start | bytes 258048 | tf_op jit(solution)/shard_map/reduce_scatter | solution.py:250
  426.0 109.8 %reduce-scatter.41.cloned.1.call-start = ((), (), s32[]{:S(2)}) async-start(), calls=%async_computation.26 | async-start | bytes 1806336 | tf_op jit(solution)/shard_map/reduce_scatter | solution.py:256
  428.9 149.3 %reduce-scatter.35.cloned.1.call-start = ((), (), s32[]{:S(2)}) async-start(), calls=%async_computation.23 | async-start | bytes 1806336 | tf_op jit(solution)/shard_map/reduce_scatter | solution.py:247
  436.0 218.7 %reduce-scatter.47.cloned.1.call-start = ((), (), s32[]{:S(2)}) async-start(), calls=%async_computation.29 | async-start | bytes 9805824 | tf_op jit(solution)/shard_map/reduce_scatter | solution.py:265
  443.7 287.3 %reduce-scatter.45.cloned.1.call-start = ((), (), s32[]{:S(2)}) async-start(), calls=%async_computation.28 | async-start | bytes 9805824 | tf_op jit(solution)/shard_map/reduce_scatter | solution.py:262
  451.4 356.0 %reduce-scatter.43.cloned.1.call-start = ((), (), s32[]{:S(2)}) async-start(), calls=%async_computation.27 | async-start | bytes 9805824 | tf_op jit(solution)/shard_map/reduce_scatter | solution.py:259
  459.1 407.8 %reduce-scatter.53.cloned.1.call-start = ((), (), s32[]{:S(2)}) async-start(), calls=%async_computation.35 | async-start | bytes 40960
  460.6 407.7 %reduce-scatter.51.cloned.1.call-start = ((), (), s32[]{:S(2)}) async-start(), calls=%async_computation.34 | async-start | bytes 40960
  495.1 374.8 %reduce-scatter.55.cloned.1.call-start = ((), (), s32[]{:S(2)}) async-start(), calls=%async_computation.36 | async-start | bytes 286720
  537.6 352.0 %reduce-scatter.49.cloned.1.call-start = ((), (), s32[]{:S(2)}) async-start(), calls=%async_computation.33 | async-start | bytes 286720
  580.0 340.4 %reduce-scatter.61.cloned.1.call-start = ((), (), s32[]{:S(2)}) async-start(), calls=%async_computation.39 | async-start | bytes 1556480
  657.0 294.8 %reduce-scatter.59.cloned.1.call-start = ((), (), s32[]{:S(2)}) async-start(), calls=%async_computation.38 | async-start | bytes 1556480
  733.4 249.6 %reduce-scatter.57.cloned.1.call-start = ((), (), s32[]{:S(2)}) async-start(), calls=%async_computation.37 | async-start | bytes 1556480
  (41 other events, 1143.5 us)
Sparse Core Ops, SparseCore 0:
  9.6 37.3 all-gather.23
  48.5 28.5 all-gather.21
  78.7 29.0 all-gather.25
  110.0 25.2 all-gather.11
  137.7 25.8 all-gather.13
  165.3 55.7 all-gather.17
  223.0 55.7 all-gather.15
  280.7 55.7 all-gather.19
  379.5 21.6 reduce-scatter.32
  403.9 19.8 reduce-scatter.30
  427.5 30.2 reduce-scatter.38
  461.6 31.9 reduce-scatter.36
  497.0 38.7 reduce-scatter.40
  539.5 38.7 reduce-scatter.34
  581.6 72.9 reduce-scatter.46
  658.0 72.9 reduce-scatter.44
  734.4 72.9 reduce-scatter.42
  809.5 18.8 reduce-scatter.52
  831.3 17.0 reduce-scatter.50
  851.1 17.6 reduce-scatter.54
  871.7 17.7 reduce-scatter.48
  891.9 28.4 reduce-scatter.60
  922.8 28.9 reduce-scatter.58
  954.0 28.9 reduce-scatter.56
where the time goes:
time: 1000 us; the launch traced here: 992 us
  waiting for transfers between devices  607 us (61%)
  blocking collectives  164 us (16%)
  matrix products  127 us (13%)
  local copies, waits for them, and re-layouts  47.1 us (5%)
  other arithmetic  29 us (3%)
  between operations  16.9 us (2%)
    unnamed x31, waiting for transfers between devices  108 us
    reduce_scatter x1, waiting for transfers between devices, on_device(): lax.psum_scatter(grad_down.astype(jnp.bfloat16), 'dp', scatter_dimension=...  74.5 us
    reduce_scatter x1, waiting for transfers between devices, on_device(): lax.psum_scatter(grad_up.astype(jnp.bfloat16), 'dp', scatter_dimension=0,...  73.9 us
    reduce_scatter x1, waiting for transfers between devices, on_device(): lax.psum_scatter(grad_gate.astype(jnp.bfloat16), 'dp', scatter_dimension=...  73.6 us
    dot_general x14, matrix products, contract(): lax.dot_general(left_mat, right_mat, (((left_dim,), (right_dim,)), ((), (...  56.9 us
    all_gather x1, waiting for transfers between devices, on_device(): lax.all_gather(down_part, 'dp', axis=1, tiled=True)  49.8 us
    reduce_scatter x1, waiting for transfers between devices, on_device(): lax.psum_scatter(grad_out.astype(jnp.bfloat16), 'dp', scatter_dimension=0...  40.7 us
    reduce_scatter x1, waiting for transfers between devices, on_device(): lax.psum_scatter(grad_query.astype(jnp.bfloat16), 'dp', scatter_dimension...  40.6 us
  transfers between devices with their start and end apart: 24, of which 17 were waited for; matrix products, arithmetic and copies ran while one was open for 16% of the time, Pallas kernels for 0%

commit v1 on v0

v1 whole, which is shorter than its diff:
```python
import jax
import jax.numpy as jnp
from jax import lax
from jax.sharding import PartitionSpec as P

H = 14
KVH = 2
HD = 64


norm_eps = 1e-06
rope_base = 1000000.0


def contract(left_mat, right_mat, left_dim, right_dim):
    return lax.dot_general(
        left_mat,
        right_mat,
        (((left_dim,), (right_dim,)), ((), ())),
        preferred_element_type=jnp.float32,
    )


def angle_tables(positions, head_dim):
    half_dim = head_dim // 2
    frequency = rope_base ** (-2.0 * jnp.arange(half_dim, dtype=jnp.float32) / head_dim)
    angles = positions.astype(jnp.float32)[:, None] * frequency[None, :]
    return (jnp.cos(angles)[:, None, :], jnp.sin(angles)[:, None, :])


def rotate(heads_field, cosine, sine_table):
    half_dim = heads_field.shape[-1] // 2
    first_half = heads_field[..., :half_dim]
    second = heads_field[..., half_dim:]
    return jnp.concatenate(
        [first_half * cosine - second * sine_table, second * cosine + first_half * sine_table],
        axis=-1,
    )


def unrotate(grad_field, cosine, sine_table):
    half_dim = grad_field.shape[-1] // 2
    first_half = grad_field[..., :half_dim]
    second = grad_field[..., half_dim:]
    return jnp.concatenate(
        [first_half * cosine + second * sine_table, second * cosine - first_half * sine_table],
        axis=-1,
    )


def score_block(query_rot, key_all, query_seg, key_seg, query_pos, key_pos):
    scores = (
        jnp.einsum("qgjd,kgd->gjqk", query_rot, key_all, preferred_element_type=jnp.float32) * 0.125
    )
    allowed = (query_seg[:, None] == key_seg[None, :]) & (query_pos[:, None] >= key_pos[None, :])
    return jnp.where(allowed, scores, -1e30)


def on_device(
    tokens,
    segments,
    cotangent,
    attn_gain,
    w_query,
    b_query,
    w_key,
    b_key,
    w_value,
    b_value,
    w_out,
    mlp_gain,
    w_gate,
    w_up,
    w_down,
):
    local_len = tokens.shape[1]
    model_width = tokens.shape[2]
    seq_count = lax.axis_size("seq")
    dp_count = lax.axis_size("dp")
    seq_place = lax.axis_index("seq")
    full_len = local_len * seq_count
    group_size = H // KVH
    kv_width = KVH * HD
    rows = w_query.shape[0]
    q_cols = w_query.shape[1]
    k_cols = w_key.shape[1]
    pack_cols = 2 * q_cols + 2 * k_cols

    def as_row(vector):
        return jnp.pad(vector, (0, pack_cols - vector.shape[0]))[None]

    packed = jnp.concatenate(
        [
            jnp.concatenate([w_query, w_out, w_key, w_value], axis=1),
            jnp.concatenate([attn_gain, b_query, b_key, b_value])[None],
            as_row(mlp_gain),
            as_row(segments[0].astype(jnp.bfloat16)),
            jnp.zeros((13, pack_cols), jnp.bfloat16),
        ],
        axis=0,
    )
    by_seq = lax.all_gather(packed, "seq", axis=0)
    attn_all = lax.all_gather(by_seq[:, :rows], "dp", axis=0)
    attn_all = attn_all.transpose(0, 2, 1, 3).reshape(model_width, seq_count, pack_cols)
    mat_query = attn_all[:, :, :q_cols].reshape(model_width, model_width)
    mat_out = attn_all[:, :, q_cols : 2 * q_cols].reshape(model_width, model_width)
    mat_key = attn_all[:, :, 2 * q_cols : 2 * q_cols + k_cols].reshape(model_width, kv_width)
    mat_value = attn_all[:, :, 2 * q_cols + k_cols :].reshape(model_width, kv_width)
    vectors = by_seq[:, rows].astype(jnp.float32)
    gain_one = vectors[:, :q_cols].reshape(model_width)
    bias_query = vectors[:, q_cols : 2 * q_cols].reshape(model_width)
    bias_key = vectors[:, 2 * q_cols : 2 * q_cols + k_cols].reshape(kv_width)
    bias_value = vectors[:, 2 * q_cols + k_cols :].reshape(kv_width)
    gain_two = by_seq[:, rows + 1, :q_cols].astype(jnp.float32).reshape(model_width)
    seg_all = by_seq[:, rows + 2, :local_len].reshape(full_len)
    seg_own = segments[0].astype(jnp.bfloat16)

    mat_gate = lax.all_gather(w_gate, "dp", axis=0, tiled=True)
    mat_up = lax.all_gather(w_up, "dp", axis=0, tiled=True)
    mat_down = lax.all_gather(w_down.T, "dp", axis=0, tiled=True)
    d_result = cotangent[0]
    d_result_all = lax.all_gather(d_result, "seq", axis=0, tiled=True)

    own_pos = seq_place * local_len + jnp.arange(local_len, dtype=jnp.int32)
    all_pos = jnp.arange(full_len, dtype=jnp.int32)
    cosine, sine_table = angle_tables(own_pos, HD)
    inputs = tokens[0].astype(jnp.float32)
    scale_one = lax.rsqrt(jnp.mean(inputs * inputs, axis=-1, keepdims=True) + norm_eps)
    normed = (inputs * scale_one * gain_one).astype(jnp.bfloat16)
    query_lin = jnp.dot(normed, mat_query, preferred_element_type=jnp.float32) + bias_query
    key_lin = jnp.dot(normed, mat_key, preferred_element_type=jnp.float32) + bias_key
    value_lin = jnp.dot(normed, mat_value, preferred_element_type=jnp.float32) + bias_value
    query_rot = rotate(query_lin.reshape(local_len, H, HD), cosine, sine_table).astype(
        jnp.bfloat16
    )
    query_rot = query_rot.reshape(local_len, KVH, group_size, HD)
    key_rot = rotate(key_lin.reshape(local_len, KVH, HD), cosine, sine_table).astype(jnp.bfloat16)
    value_loc = value_lin.astype(jnp.bfloat16)
    kv_loc = jnp.concatenate([key_rot.reshape(local_len, kv_width), value_loc], axis=1)
    kv_all = lax.all_gather(kv_loc, "seq", axis=0, tiled=True)
    key_all = kv_all[:, :kv_width].reshape(full_len, KVH, HD)
    value_all = kv_all[:, kv_width:].reshape(full_len, KVH, HD)
    masked = score_block(query_rot, key_all, seg_own, seg_all, own_pos, all_pos)
    highest = jnp.max(masked, axis=-1, keepdims=True)
    weights = jnp.exp(masked - highest)
    totals = jnp.sum(weights, axis=-1, keepdims=True)
    prob_low = (weights / totals).astype(jnp.bfloat16)
    log_total = highest + jnp.log(totals)
    mixed = jnp.einsum("gjqk,kgd->qgjd", prob_low, value_all, preferred_element_type=jnp.float32)
    mixed = mixed.astype(jnp.bfloat16).reshape(local_len, model_width)
    residual = inputs + jnp.dot(mixed, mat_out, preferred_element_type=jnp.float32)
    scale_two = lax.rsqrt(jnp.mean(residual * residual, axis=-1, keepdims=True) + norm_eps)
    normed_loc = (residual * scale_two * gain_two).astype(jnp.bfloat16)

    normed_two = lax.all_gather(normed_loc, "seq", axis=0, tiled=True)
    gate_lin = jnp.dot(normed_two, mat_gate, preferred_element_type=jnp.float32)
    up_lin = jnp.dot(normed_two, mat_up, preferred_element_type=jnp.float32)
    d_hidden = jnp.dot(d_result_all, mat_down, preferred_element_type=jnp.float32)
    sigmoid_gate = 1.0 / (1.0 + jnp.exp(-gate_lin))
    silu_gate = gate_lin * sigmoid_gate
    hidden = (silu_gate * up_lin).astype(jnp.bfloat16)
    d_gate = (
        d_hidden * up_lin * (sigmoid_gate + gate_lin * sigmoid_gate * (1.0 - sigmoid_gate))
    ).astype(jnp.bfloat16)
    d_up = (d_hidden * silu_gate).astype(jnp.bfloat16)
    d_norm_all = (contract(d_gate, mat_gate, 1, 1) + contract(d_up, mat_up, 1, 1)).astype(
        jnp.bfloat16
    )
    d_norm_part = lax.psum_scatter(d_norm_all, "seq", scatter_dimension=0, tiled=True).astype(
        jnp.float32
    )
    branch_all = contract(hidden, mat_down, 1, 1).astype(jnp.bfloat16)
    branch_sum = lax.psum_scatter(branch_all, "seq", scatter_dimension=0, tiled=True)
    output = (residual + branch_sum.astype(jnp.float32)).astype(jnp.bfloat16)[None]
    grad_gate, grad_up, grad_down = (
        lax.psum_scatter(
            contract(left, right, 0, 0).astype(jnp.bfloat16), "dp", scatter_dimension=0, tiled=True
        ).astype(jnp.float32)
        for left, right in ((normed_two, d_gate), (normed_two, d_up), (d_result_all, hidden))
    )

    grad_gain_two = jnp.sum(d_norm_part * residual * scale_two, axis=0)
    d_scaled_two = d_norm_part * gain_two
    d_residual = (
        d_result.astype(jnp.float32)
        + scale_two * d_scaled_two
        - residual * scale_two**3 * jnp.mean(d_scaled_two * residual, axis=-1, keepdims=True)
    )
    d_attn = d_residual.astype(jnp.bfloat16)
    grad_out = contract(mixed, d_attn, 0, 0)
    d_mixed = (
        contract(d_attn, mat_out, 1, 1)
        .astype(jnp.bfloat16)
        .reshape(local_len, KVH, group_size, HD)
    )
    masked = score_block(query_rot, key_all, seg_own, seg_all, own_pos, all_pos)
    prob_full = jnp.exp(masked - log_total)
    prob_low = prob_full.astype(jnp.bfloat16)
    d_probs = jnp.einsum("qgjd,kgd->gjqk", d_mixed, value_all, preferred_element_type=jnp.float32)
    d_value_full = jnp.einsum(
        "gjqk,qgjd->kgd", prob_low, d_mixed, preferred_element_type=jnp.float32
    )
    d_scores = (
        prob_full * (d_probs - jnp.sum(d_probs * prob_full, axis=-1, keepdims=True))
    ).astype(jnp.bfloat16)
    d_key_full = (
        jnp.einsum("gjqk,qgjd->kgd", d_scores, query_rot, preferred_element_type=jnp.float32)
        * 0.125
    )
    d_kv_full = jnp.concatenate(
        [d_key_full.reshape(full_len, kv_width), d_value_full.reshape(full_len, kv_width)], axis=1
    ).astype(jnp.bfloat16)
    d_kv_loc = lax.psum_scatter(d_kv_full, "seq", scatter_dimension=0, tiled=True)
    d_query_rot = (
        jnp.einsum("gjqk,kgd->qgjd", d_scores, key_all, preferred_element_type=jnp.float32) * 0.125
    ).reshape(local_len, H, HD)
    d_query_lin = (
        unrotate(d_query_rot, cosine, sine_table)
        .astype(jnp.bfloat16)
        .reshape(local_len, model_width)
    )
    d_key_loc = d_kv_loc[:, :kv_width].astype(jnp.float32).reshape(local_len, KVH, HD)
    d_key_lin = (
        unrotate(d_key_loc, cosine, sine_table).astype(jnp.bfloat16).reshape(local_len, kv_width)
    )
    d_value_lin = d_kv_loc[:, kv_width:]
    grad_query = contract(normed, d_query_lin, 0, 0)
    grad_key = contract(normed, d_key_lin, 0, 0)
    grad_value = contract(normed, d_value_lin, 0, 0)

    attn_grads = jnp.concatenate(
        [
            item.astype(jnp.bfloat16).reshape(dp_count, rows, seq_count, -1)
            for item in (grad_query, grad_out, grad_key, grad_value)
        ],
        axis=3,
    ).transpose(0, 2, 1, 3)
    attn_grads = lax.psum_scatter(attn_grads, "dp", scatter_dimension=0)
    attn_grads = lax.psum_scatter(attn_grads, "seq", scatter_dimension=0).astype(jnp.float32)

    grad_bias_query = jnp.sum(d_query_lin, axis=0, dtype=jnp.float32)
    grad_bias_key = jnp.sum(d_key_lin, axis=0, dtype=jnp.float32)
    grad_bias_value = jnp.sum(d_value_lin, axis=0, dtype=jnp.float32)
    d_normed = (
        contract(d_query_lin, mat_query, 1, 1)
        + contract(d_key_lin, mat_key, 1, 1)
        + contract(d_value_lin, mat_value, 1, 1)
    )
    grad_gain_one = jnp.sum(d_normed * inputs * scale_one, axis=0)
    d_scaled = d_normed * gain_one
    d_inputs = (
        d_residual
        + scale_one * d_scaled
        - inputs * scale_one**3 * jnp.mean(d_scaled * inputs, axis=-1, keepdims=True)
    )
    small = jnp.concatenate(
        [
            item.reshape(seq_count, -1)
            for item in (
                grad_gain_one,
                grad_bias_query,
                grad_gain_two,
                grad_bias_key,
                grad_bias_value,
            )
        ],
        axis=1,
    )
    small = lax.psum(small, ("dp", "seq"))
    small = lax.dynamic_index_in_dim(small, seq_place, 0, keepdims=False)
    return (
        output,
        d_inputs[None],
        small[:q_cols],
        attn_grads[:, :q_cols],
        small[q_cols : 2 * q_cols],
        attn_grads[:, 2 * q_cols : 2 * q_cols + k_cols],
        small[3 * q_cols : 3 * q_cols + k_cols],
        attn_grads[:, 2 * q_cols + k_cols :],
        small[3 * q_cols + k_cols :],
        attn_grads[:, q_cols : 2 * q_cols],
        small[2 * q_cols : 3 * q_cols],
        grad_gate,
        grad_up,
        grad_down.T,
    )


def solution(mesh):
    return jax.shard_map(
        on_device,
        mesh=mesh,
        in_specs=(
            P("dp", "seq", None),
            P("dp", "seq"),
            P("dp", "seq", None),
            P("seq"),
            P("dp", "seq"),
            P("seq"),
            P("dp", "seq"),
            P("seq"),
            P("dp", "seq"),
            P("seq"),
            P("dp", "seq"),
            P("seq"),
            P("dp", "seq"),
            P("dp", "seq"),
            P("seq", "dp"),
        ),
        out_specs=(
            P("dp", "seq", None),
            P("dp", "seq", None),
            P("seq"),
            P("dp", "seq"),
            P("seq"),
            P("dp", "seq"),
            P("seq"),
            P("dp", "seq"),
            P("seq"),
            P("dp", "seq"),
            P("seq"),
            P("dp", "seq"),
            P("dp", "seq"),
            P("seq", "dp"),
        ),
        check_vma=False,
    )
```

time: 1000 us -> 685 us (0.69)
  waiting for transfers between devices: 607 us -> 364 us
  blocking collectives: 164 us -> 73 us
  other arithmetic: 29 us -> 41.9 us
    reduce_scatter x9 -> x7, waiting for transfers between devices: 362 us -> 202 us  [the longest x2 83.3 us: on_device(): lax.psum_scatter(contract(left, right, 0, 0).astype(jnp.bfloat16), 'dp',...]
    unnamed x31 -> x15, waiting for transfers between devices: 108 us -> 2.46 us
    all_gather x9 -> x2, blocking collectives: 114 us -> 33.4 us  [the longest x1 17.4 us: on_device(): by_seq = lax.all_gather(packed, 'seq', axis=0)]
    all_gather x8 -> x6, waiting for transfers between devices: 137 us -> 160 us  [the longest x1 39.9 us: on_device(): normed_two = lax.all_gather(normed_loc, 'seq', axis=0, tiled=True)]
    unnamed x114 -> x91, local copies, waits for them, and re-layouts: 33.7 us -> 13.5 us
    reshape x0 -> x13, local copies, waits for them, and re-layouts: none -> 19.5 us  [the longest x8 19.1 us: on_device(): item.astype(jnp.bfloat16).reshape(dp_count, rows, seq_count, -1)]
    slice x0 -> x16, local copies, waits for them, and re-layouts: none -> 15.9 us  [the longest x2 5.73 us: on_device(): attn_all[:, :, q_cols:2 * q_cols].reshape(model_width, model_width)]
    unnamed x1 -> x0, blocking collectives: 10.4 us -> none
  transfers between devices with their start and end apart: 24 -> 14, of which waited for: 17 -> 10; matrix products, arithmetic and copies ran while one was open for 16% -> 22% of each run, Pallas kernels for 0% -> 0%
where the time goes in v1:
time: 685 us; the launch traced here: 675 us
  waiting for transfers between devices  364 us (53%)
  matrix products  123 us (18%)
  blocking collectives  73 us (11%)
  local copies, waits for them, and re-layouts  56.8 us (8%)
  other arithmetic  41.9 us (6%)
  between operations  15.1 us (2%)
    reduce_scatter x2, waiting for transfers between devices, on_device(): lax.psum_scatter(contract(left, right, 0, 0).astype(jnp.bfloat16), 'dp',...  83.3 us
    dot_general x14, matrix products, contract(): lax.dot_general(left_mat, right_mat, (((left_dim,), (right_dim,)), ((), (...  53 us
    reduce_scatter x1, waiting for transfers between devices, on_device(): attn_grads = lax.psum_scatter(attn_grads, 'dp', scatter_dimension=0)  45.8 us
    all_gather x1, waiting for transfers between devices, on_device(): normed_two = lax.all_gather(normed_loc, 'seq', axis=0, tiled=True)  39.9 us
    reduce_scatter x1, waiting for transfers between devices, on_device(): lax.psum_scatter(branch_all, 'seq', scatter_dimension=0, tiled=True)  39.6 us
    psum x1, blocking collectives, on_device(): small = lax.psum(small, ('dp', 'seq'))  39.6 us
    all_gather x1, waiting for transfers between devices, on_device(): d_result_all = lax.all_gather(d_result, 'seq', axis=0, tiled=True)  35.7 us
    all_gather x1, waiting for transfers between devices, on_device(): attn_all = lax.all_gather(by_seq[:, :rows], 'dp', axis=0)  33 us
  transfers between devices with their start and end apart: 14, of which 10 were waited for; matrix products, arithmetic and copies ran while one was open for 22% of the time, Pallas kernels for 0%

profile of v1, /device:TPU:0, one launch (start us, length us, event | category | flops | bytes accessed | tf_op | source)
XLA Modules:
  0.0 675.3 jit_solution(7380740370688884596)
XLA Ops:
  12.2 17.4 %all-gather = bf16[512,512]{1,0:T(8,128)(2,1)S(1)} all-gather(bf16[128,512]{1,0:T(8,128)(2,1)S(1)} %concatenate.45), channel_id=2, replica_groups=mesh['dp'=8,'seq'=4] {'seq'}, dimensions={0}, use_global_device_ids=true | all-gather | bytes 655360 | tf_op jit(solution)/shard_map/all_gather | solution.py:102
  33.8 33.0 %all-gather.18.cloned.1.call-done = bf16[32,112,512]{2,1,0:T(8,128)(2,1)} async-done(((bf16[4,112,512]{2,1,0:T(8,128)(2,1)}), bf16[32,112,512]{2,1,0:T(8,128)(2,1)}) %all-gather.18.cloned.1.call-update) | async-done | bytes 3670032 | tf_op jit(solution)/shard_map/all_gather | solution.py:103
  77.6 16.1 %all_gather.34 = bf16[1024,256]{0,1:T(8,128)(2,1)S(1)} all-gather(bf16[256,256]{0,1:T(8,128)(2,1)S(1)} %pad_maximum_fusion.5), channel_id=1, replica_groups=mesh['dp'=8,'seq'=4] {'seq'}, dimensions={0}, use_global_device_ids=true | all-gather | bytes 655360 | tf_op jit(solution)/shard_map/all_gather | solution.py:140
  102.8 7.6 %fusion.74 = (f32[2,7,256]{2,1,0:T(8,128)S(1)}, f32[2,7,256,1024]{2,3,1,0:T(8,128)}) fusion(bf16[1024,2,64,1]{0,2,3,1:T(8,128)(2,1)S(1)} %bitcast.199, bf16[256,2,7,32]{0,3,2,1:T(8,128)(2,1)S(1)} %bitcast.203, bf16[256,2,7,32]{0,3,2,1:T(8,128)(2,1)S(1)} %bitcast.201, pred[256,1024]{0,1:T(8,128)(4,1)} %fusion.31), kind=kOutput, calls=%fused_computation.140 | convolution fusion | flops 481686016 | bytes 15677440 | tf_op jit(solution)/shard_map/qgjd,kgd->gjqk/dot_general | solution.py:53
  110.4 7.1 %fusion.3 = f32[2,7,256]{2,1,0:T(8,128)S(1)} fusion(f32[2,7,256,1024]{2,3,1,0:T(8,128)} %get-tuple-element.113, f32[2,7,256]{2,1,0:T(8,128)S(1)} %get-tuple-element.112), kind=kLoop, calls=%fused_computation.9 | loop fusion | flops 7336448 | bytes 14708736 | tf_op jit(solution)/shard_map/reduce_sum | solution.py:146
  117.6 6.6 fusion.14
  128.7 39.9 %all-gather.10.cloned.1.call-done = bf16[1024,896]{1,0:T(8,128)(2,1)} async-done(((bf16[256,896]{1,0:T(8,128)(2,1)}), bf16[1024,896]{1,0:T(8,128)(2,1)}) %all-gather.10.cloned.1.call-update) | async-done | bytes 1835024 | tf_op jit(solution)/shard_map/all_gather | solution.py:155
  168.6 7.2 %fusion.76 = f32[1024,1216]{0,1:T(8,128)} fusion(bf16[1024,896]{1,0:T(8,128)(2,1)} %all-gather.10.cloned.1.call-done, bf16[896,1216]{1,0:T(8,128)(2,1)} %all-gather.14.cloned.1.call-done), kind=kOutput, calls=%fused_computation.142 | convolution fusion | flops 2231369728 | bytes 8994816 | tf_op jit(solution)/shard_map/dot_general | solution.py:157
  175.8 22.2 %all-gather.12.cloned.1.call-done = bf16[896,1216]{1,0:T(8,128)(2,1)} async-done(((bf16[112,1216]{1,0:T(8,128)(2,1)}), bf16[896,1216]{1,0:T(8,128)(2,1)}) %all-gather.12.cloned.1.call-update) | async-done | bytes 2179088 | tf_op jit(solution)/shard_map/all_gather | solution.py:118
  198.0 7.2 %fusion.75 = f32[1024,1216]{0,1:T(8,128)} fusion(bf16[1024,896]{1,0:T(8,128)(2,1)} %all-gather.10.cloned.1.call-done, bf16[896,1216]{1,0:T(8,128)(2,1)} %all-gather.12.cloned.1.call-done), kind=kOutput, calls=%fused_computation.141 | convolution fusion | flops 2231369728 | bytes 8994816 | tf_op jit(solution)/shard_map/dot_general | solution.py:156
  205.1 35.7 %all-gather.20.cloned.1.call-done = bf16[1,1024,896]{2,1,0:T(8,128)(2,1)} async-done(((bf16[1,256,896]{2,1,0:T(8,128)(2,1)}), bf16[1,1024,896]{2,1,0:T(8,128)(2,1)}) %all-gather.20.cloned.1.call-update) | async-done | bytes 1835024 | tf_op jit(solution)/shard_map/all_gather | solution.py:122
  240.8 29.4 %all-gather.16.cloned.1.call-done = bf16[896,1216]{1,0:T(8,128)(2,1)} async-done(((bf16[112,1216]{1,0:T(8,128)(2,1)}), bf16[896,1216]{1,0:T(8,128)(2,1)}) %all-gather.16.cloned.1.call-update) | async-done | bytes 2179088 | tf_op jit(solution)/shard_map/all_gather | solution.py:120
  270.2 11.4 %multiply_convert_fusion = (bf16[1024,1216]{0,1:T(8,128)(2,1)S(1)}, bf16[1024,1216]{0,1:T(8,128)(2,1)S(1)}, bf16[1024,1216]{0,1:T(8,128)(2,1)}) fusion(f32[1024,1216]{0,1:T(8,128)} %fusion.75, f32[1024,1216]{0,1:T(8,128)} %fusion.76, bf16[896,1216]{1,0:T(8,128)(2,1)} %all-gather.16.cloned.1.call-done, bf16[1,1024,896]{2,1,0:T(8,128)(2,1)} %all-gather.20.cloned.1.call-done), kind=kOutput, calls=%fused_computation.14 | convolution fusion | flops 2248802304 | bytes 21446656 | tf_op jit(solution)/shard_map/dot_general | solution.py:158
  281.6 13.6 %fusion.77 = f32[1024,896]{1,0:T(8,128)S(1)} fusion(bf16[1024,1216]{0,1:T(8,128)(2,1)S(1)} %get-tuple-element.75, bf16[896,1216]{1,0:T(8,128)(2,1)S(1)} %copy-done.33), kind=kOutput, calls=%fused_computation.143 | convolution fusion | flops 2231369728 | bytes 8339456 | tf_op jit(solution)/shard_map/dot_general | solution.py:16
  299.5 6.6 convolution_convert_fusion.3
  306.2 32.8 %reduce-scatter.13.cloned.1.call-done = bf16[256,896]{1,0:T(8,128)(2,1)} async-done(((bf16[1024,896]{1,0:T(8,128)(2,1)}), bf16[256,896]{1,0:T(8,128)(2,1)}) %reduce-scatter.13.cloned.1.call-update) | async-done | bytes 458768 | tf_op jit(solution)/shard_map/reduce_scatter | solution.py:169
  340.4 39.6 %reduce-scatter.11.cloned.1.call-done = bf16[256,896]{1,0:T(8,128)(2,1)} async-done(((bf16[1024,896]{1,0:T(8,128)(2,1)}), bf16[256,896]{1,0:T(8,128)(2,1)}) %reduce-scatter.11.cloned.1.call-update) | async-done | bytes 458768 | tf_op jit(solution)/shard_map/reduce_scatter | solution.py:173
  383.3 7.7 %fusion.20 = bf16[2,64,1024]{2,1,0:T(8,128)(2,1)S(1)} fusion(bf16[256,2,7,64]{0,3,2,1:T(8,128)(2,1)S(1)} %bitcast.192, f32[2,7,256,1024]{2,3,1,0:T(8,128)} %get-tuple-element.113, f32[2,7,256]{2,1,0:T(8,128)S(1)} %log_add_fusion), kind=kOutput, calls=%fused_computation.42 | convolution fusion | flops 477233152 | bytes 15415296 | tf_op jit(solution)/shard_map/gjqk,qgjd->kgd/dot_general | solution.py:200
  391.0 10.9 %fusion = (f32[2,7,256]{2,1,0:T(8,128)S(1)}, f32[2,1024,256,7]{2,1,3,0:T(8,128)}) fusion(f32[2,7,256,1024]{2,3,1,0:T(8,128)} %get-tuple-element.113, f32[2,7,256]{2,1,0:T(8,128)S(1)} %log_add_fusion, bf16[1024,2,64,1]{0,2,3,1:T(8,128)(2,1)S(1)} %bitcast.212, bf16[256,2,7,64]{0,3,2,1:T(8,128)(2,1)S(1)} %bitcast.193), kind=kOutput, calls=%fused_computation.2 | convolution fusion | flops 480768512 | bytes 30109696 | tf_op jit(solution)/shard_map/qgjd,kgd->gjqk/dot_general | solution.py:199
  402.0 7.2 %fusion.2 = bf16[2,7,256,1024]{2,3,1,0:T(8,128)(2,1)S(1)} fusion(f32[2,1024,256,7]{2,1,3,0:T(8,128)} %get-tuple-element.117, f32[2,7,256,1024]{2,3,1,0:T(8,128)S(1)} %bitcast.185, f32[2,7,256]{2,1,0:T(8,128)S(1)} %get-tuple-element.116, f32[2,7,256]{2,1,0:T(8,128)S(1)} %log_add_fusion), kind=kLoop, calls=%fused_computation.4 | loop fusion | flops 14680064 | bytes 36728832 | tf_op jit(solution)/shard_map/convert_element_type | solution.py:205
  483.8 39.7 %reduce-scatter.23.cloned.1.call-done = bf16[112,1216]{1,0:T(8,128)(2,1)} async-done(((bf16[896,1216]{1,0:T(8,128)(2,1)}), bf16[112,1216]{1,0:T(8,128)(2,1)}) %reduce-scatter.23.cloned.1.call-update) | async-done | bytes 272400 | tf_op jit(solution)/shard_map/reduce_scatter | solution.py:176
  525.3 43.6 %reduce-scatter.21.cloned.1.call-done = bf16[112,1216]{1,0:T(8,128)(2,1)} async-done(((bf16[896,1216]{1,0:T(8,128)(2,1)}), bf16[112,1216]{1,0:T(8,128)(2,1)}) %reduce-scatter.21.cloned.1.call-update) | async-done | bytes 272400 | tf_op jit(solution)/shard_map/reduce_scatter | solution.py:176
  575.7 45.8 %reduce-scatter.17.cloned.1.call-done = bf16[1,4,112,512]{3,2,1,0:T(8,128)(2,1)} async-done(((bf16[8,4,112,512]{3,2,1,0:T(8,128)(2,1)}), bf16[1,4,112,512]{3,2,1,0:T(8,128)(2,1)}) %reduce-scatter.17.cloned.1.call-update) | async-done | bytes 458768 | tf_op jit(solution)/shard_map/reduce_scatter | solution.py:238
  623.3 39.6 %psum.7 = f32[4,736]{1,0:T(4,128)S(1)} all-reduce(f32[4,736]{1,0:T(4,128)S(1)} %concatenate.54), channel_id=1, replica_groups=mesh['dp'=8,'seq'=4] {'dp','seq'}, use_global_device_ids=true, to_apply=%region_15.16 | all-reduce | flops 2944 | bytes 23552 | tf_op jit(solution)/shard_map/psum | solution.py:269
  (227 shorter events, 132.5 us)
Async XLA Ops:
  7.2 24.3 %copy-start.1 = (bf16[1,256,896]{2,1,0:T(8,128)(2,1)S(1)}, bf16[1,256,896]{2,1,0:T(8,128)(2,1)}, u32[]{:S(2)}) copy-start(bf16[1,256,896]{2,1,0:T(8,128)(2,1)} %param.15) | copy-start | bytes 1376260
  7.2 59.7 %all-gather.18.cloned.1.call-start = ((), (), s32[]{:S(2)}) async-start(), calls=%async_computation.19 | async-start | bytes 4128768 | tf_op jit(solution)/shard_map/all_gather | solution.py:103
  30.4 98.2 %all-gather.14.cloned.1.call-start = ((), (), s32[]{:S(2)}) async-start(), calls=%async_computation.10 | async-start | bytes 2580480 | tf_op jit(solution)/shard_map/all_gather | solution.py:119
  31.2 137.4 %all-gather.10.cloned.1.call-start = ((), (), s32[]{:S(2)}) async-start(), calls=%async_computation.8 | async-start | bytes 2293760 | tf_op jit(solution)/shard_map/all_gather | solution.py:155
  125.6 213.4 %copy-start.30 = (f32[256]{0:T(256)}, f32[256]{0:T(256)S(1)}, u32[]{:S(2)}) copy-start(f32[256]{0:T(256)S(1)} %get-tuple-element.111) | copy-start | bytes 3076
  126.6 71.4 %all-gather.12.cloned.1.call-start = ((), (), s32[]{:S(2)}) async-start(), calls=%async_computation.9 | async-start | bytes 2580480 | tf_op jit(solution)/shard_map/all_gather | solution.py:118
  127.2 113.6 %all-gather.20.cloned.1.call-start = ((), (), s32[]{:S(2)}) async-start(), calls=%async_computation.20 | async-start | bytes 2293760 | tf_op jit(solution)/shard_map/all_gather | solution.py:122
  127.8 142.4 %all-gather.16.cloned.1.call-start = ((), (), s32[]{:S(2)}) async-start(), calls=%async_computation.11 | async-start | bytes 2580480 | tf_op jit(solution)/shard_map/all_gather | solution.py:120
  128.3 210.7 %reduce-scatter.13.cloned.1.call-start = ((), (), s32[]{:S(2)}) async-start(), calls=%async_computation.13 | async-start | bytes 2293760 | tf_op jit(solution)/shard_map/reduce_scatter | solution.py:169
  299.5 80.5 %reduce-scatter.11.cloned.1.call-start = ((), (), s32[]{:S(2)}) async-start(), calls=%async_computation.12 | async-start | bytes 2293760 | tf_op jit(solution)/shard_map/reduce_scatter | solution.py:173
  306.2 149.9 %reduce-scatter.15.cloned.1.call-start = ((), (), s32[]{:S(2)}) async-start(), calls=%async_computation.14 | async-start | bytes 655360 | tf_op jit(solution)/shard_map/reduce_scatter | solution.py:213
  383.3 18.6 %slice-start = ((s8[14680064]{0:T(1024)(128)(4,1)}), s8[4194304]{0:T(1024)(128)(4,1)S(1)}, s32[]{:S(2)}) async-start(s8[14680064]{0:T(1024)(128)(4,1)} %bitcast.184), calls=%async_computation.22 | async-start | bytes 8388608
  383.3 18.6 %slice-start.1 = ((s8[14680064]{0:T(1024)(128)(4,1)}), s8[4194304]{0:T(1024)(128)(4,1)S(1)}, s32[]{:S(2)}) async-start(s8[14680064]{0:T(1024)(128)(4,1)} %bitcast.184), calls=%async_computation.23 | async-start | bytes 8388608
  412.9 64.9 %reduce-scatter.25.cloned.1.call-start = ((), (), s32[]{:S(2)}) async-start(), calls=%async_computation.21 | async-start | bytes 2580480
  420.6 102.9 %reduce-scatter.23.cloned.1.call-start = ((), (), s32[]{:S(2)}) async-start(), calls=%async_computation.18 | async-start | bytes 2580480 | tf_op jit(solution)/shard_map/reduce_scatter | solution.py:176
  427.3 141.7 %reduce-scatter.21.cloned.1.call-start = ((), (), s32[]{:S(2)}) async-start(), calls=%async_computation.17 | async-start | bytes 2580480 | tf_op jit(solution)/shard_map/reduce_scatter | solution.py:176
  433.0 188.5 %reduce-scatter.17.cloned.1.call-start = ((), (), s32[]{:S(2)}) async-start(), calls=%async_computation.15 | async-start | bytes 4128768 | tf_op jit(solution)/shard_map/reduce_scatter | solution.py:238
  477.7 94.4 %copy-start.4 = (bf16[896,4,224]{0,2,1:T(8,128)(2,1)S(1)}, bf16[896,4,224]{0,2,1:T(8,128)(2,1)}, u32[]{:S(2)}) copy-start(bf16[896,4,224]{0,2,1:T(8,128)(2,1)} %copy.101) | copy-start | bytes 4816900
  477.8 94.4 %copy-start.6 = (bf16[256,14,64]{0,2,1:T(8,128)(2,1)S(1)}, bf16[256,14,64]{0,2,1:T(8,128)(2,1)}, u32[]{:S(2)}) copy-start(bf16[256,14,64]{0,2,1:T(8,128)(2,1)} %copy-done.5) | copy-start | bytes 1376260
  477.8 187.5 %reduce-scatter.19.cloned.1.call-start = ((), (), s32[]{:S(2)}) async-start(), calls=%async_computation.16 | async-start | bytes 573440 | tf_op jit(solution)/shard_map/reduce_scatter | solution.py:239
  573.8 47.7 %copy-start.20 = (bf16[896,4,32]{0,2,1:T(8,128)(2,1)S(1)}, bf16[896,4,32]{0,2,1:T(8,128)(2,1)}, u32[]{:S(2)}) copy-start(bf16[896,4,32]{0,2,1:T(8,128)(2,1)} %copy-done.19) | copy-start | bytes 688132
  574.0 49.0 %copy-start.24 = (bf16[256,2,32]{0,2,1:T(8,128)(2,1)S(1)}, bf16[256,2,32]{0,2,1:T(8,128)(2,1)}, u32[]{:S(2)}) copy-start(bf16[256,2,32]{0,2,1:T(8,128)(2,1)} %copy-done.23) | copy-start | bytes 98308
  574.0 49.0 %copy-start.26 = (bf16[256,2,32]{0,2,1:T(8,128)(2,1)S(1)}, bf16[256,2,32]{0,2,1:T(8,128)(2,1)}, u32[]{:S(2)}) copy-start(bf16[256,2,32]{0,2,1:T(8,128)(2,1)} %copy-done.25) | copy-start | bytes 98308
  574.0 90.1 %copy-start.31 = (f32[256]{0:T(256)S(1)}, f32[256]{0:T(256)}, u32[]{:S(2)}) copy-start(f32[256]{0:T(256)} %get-tuple-element.108) | copy-start | bytes 3076
  (31 other events, 177.9 us)
Sparse Core Ops, SparseCore 0:
  30.5 36.2 all-gather.17
  68.7 28.7 all-gather.13
  126.7 41.8 all-gather.9
  170.3 27.5 all-gather.11
  199.4 41.3 all-gather.19
  242.5 27.5 all-gather.15
  299.6 39.4 reduce-scatter.12
  341.4 38.5 reduce-scatter.10
  413.1 20.7 reduce-scatter.14
  437.0 40.4 reduce-scatter.24
  481.3 42.1 reduce-scatter.22
  526.7 42.1 reduce-scatter.20
  572.7 48.6 reduce-scatter.16
  623.6 20.9 reduce-scatter.18

commit v2 on v1

--- a/solution.py
+++ b/solution.py
@@ -1,6 +1,10 @@
+import functools
+
 import jax
 import jax.numpy as jnp
 from jax import lax
+from jax.experimental import pallas as pl
+from jax.experimental.pallas import tpu as pltpu
 from jax.sharding import PartitionSpec as P
 
 H = 14
@@ -54,6 +58,302 @@
     )
     allowed = (query_seg[:, None] == key_seg[None, :]) & (query_pos[:, None] >= key_pos[None, :])
     return jnp.where(allowed, scores, -1e30)
+
+
+MESH = pl.DeviceIdType.MESH
+VMEM_BYTES = 56 * 1024 * 1024
+
+
+def places(seq_count, chip_count):
+    d, s = lax.axis_index("dp"), lax.axis_index("seq")
+    chip = lax.div(d, 2)
+    core = d - 2 * chip
+    sibling = (d + 1 - 2 * core, s)
+    chips = [lax.rem(chip + k, chip_count) for k in range(chip_count)]
+    seqs = [lax.rem(s + k, seq_count) for k in range(seq_count)]
+    return d, s, chip, core, sibling, chips, seqs
+
+
+def greet(partners):
+    barrier = pltpu.get_barrier_semaphore()
+    for partner in partners:
+        pl.semaphore_signal(barrier, inc=1, device_id=partner, device_id_type=MESH)
+    pl.semaphore_wait(barrier, len(partners))
+
+
+def push(source, target, send_sem, recv_sem, device):
+    copy = pltpu.make_async_remote_copy(
+        src_ref=source,
+        dst_ref=target,
+        send_sem=send_sem,
+        recv_sem=recv_sem,
+        device_id=device,
+        device_id_type=MESH,
+    )
+    copy.start()
+    return copy
+
+
+def gather_kernel(
+    S, C, attn, vec, dy, gate, up, down,
+    attn_all, vec_all, dy_all, gate_all, up_all, down_all,
+    own_sem, s_send, s_recv, c_send, c_recv, p_send, p_recv,
+):
+    d, s, chip, core, sibling, chips, seqs = places(S, C)
+    greet(
+        [(d, seqs[k]) for k in range(1, S)]
+        + [(2 * chips[k] + core, s) for k in range(1, C)]
+        + [sibling]
+    )
+    seq_items = [(attn, attn_all.at[d, s]), (vec, vec_all.at[s]), (dy, dy_all.at[s])]
+    seq_copies = []
+    for i, (source, target) in enumerate(seq_items):
+        seq_copies.append(
+            [
+                push(source, target, s_send.at[i, k], s_recv.at[i, k], (d, seqs[k]))
+                for k in range(1, S)
+            ]
+        )
+    dp_items = [(gate, gate_all), (up, up_all), (down, down_all)]
+    own = []
+    for i, (source, target) in enumerate(
+        seq_items + [(source, whole.at[d]) for source, whole in dp_items]
+    ):
+        copy = pltpu.make_async_copy(source, target, own_sem.at[i])
+        copy.start()
+        own.append(copy)
+
+    def spread(j, source, whole):
+        far = [
+            push(source, whole.at[d], c_send.at[j, k], c_recv.at[j, k], (2 * chips[k] + core, s))
+            for k in range(1, C)
+        ]
+        near = push(source, whole.at[d], p_send.at[j, 0], p_recv.at[j, 0], sibling)
+        return far, near
+
+    copies = [spread(j, *item) for j, item in enumerate(dp_items)]
+    own[0].wait()
+    for copy in seq_copies[0]:
+        copy.wait_recv()
+    copies.append(spread(3, attn_all.at[d], attn_all))
+    wholes = [gate_all, up_all, down_all, attn_all]
+    near_copies = []
+    for j in range(4):
+        near_copies.append(copies[j][1])
+        for k in range(1, C):
+            copies[j][0][k - 1].wait_recv()
+            slot = 2 * lax.rem(chip - k + C, C) + core
+            block = wholes[j].at[slot]
+            near_copies.append(push(block, block, p_send.at[j, k], p_recv.at[j, k], sibling))
+    for copy in own[1:]:
+        copy.wait()
+    for copy in seq_copies[0]:
+        copy.wait_send()
+    for group in seq_copies[1:]:
+        for copy in group:
+            copy.wait()
+    for far, _ in copies:
+        for copy in far:
+            copy.wait_send()
+    for copy in near_copies:
+        copy.wait()
+
+
+def gather_all(S, DP, attn, vec, dy, gate, up, down):
+    C = DP // 2
+
+    def out(*shape):
+        return jax.ShapeDtypeStruct(shape, jnp.bfloat16)
+
+    dma = pltpu.SemaphoreType.DMA
+    return pl.pallas_call(
+        functools.partial(gather_kernel, S, C),
+        out_shape=[
+            out(DP, S, *attn.shape),
+            out(S, *vec.shape),
+            out(S, *dy.shape),
+            out(DP, *gate.shape),
+            out(DP, *up.shape),
+            out(DP, *down.shape),
+        ],
+        in_specs=[pl.BlockSpec(memory_space=pl.ANY)] * 6,
+        out_specs=[pl.BlockSpec(memory_space=pl.ANY)] * 6,
+        scratch_shapes=[
+            dma((6,)),
+            dma((3, S)),
+            dma((3, S)),
+            dma((4, C)),
+            dma((4, C)),
+            dma((4, C)),
+            dma((4, C)),
+        ],
+        compiler_params=pltpu.CompilerParams(
+            collective_id=0, has_side_effects=True, vmem_limit_bytes=VMEM_BYTES
+        ),
+    )(attn, vec, dy, gate, up, down)
+
+
+def scatter_kernel(
+    S, C, attn, gate, up, down, small,
+    o_attn, o_gate, o_up, o_down, o_small,
+    attn_sib, gate_sib, up_sib, down_sib,
+    attn_sum, gate_sum, up_sum, down_sum,
+    attn_far, gate_far, up_far, down_far,
+    seq_part, seq_far, small_seq, small_own, small_sib, small_chip,
+    n_send, n_recv, c_send, c_recv, s_send, s_recv, m_send, m_recv,
+):
+    d, s, chip, core, sibling, chips, seqs = places(S, C)
+    greet(
+        [(d, seqs[k]) for k in range(1, S)]
+        + [(2 * chips[k] + core, s) for k in range(1, C)]
+        + [sibling]
+    )
+    items = [
+        (attn, attn_sib, attn_sum, attn_far),
+        (gate, gate_sib, gate_sum, gate_far),
+        (up, up_sib, up_sum, up_far),
+        (down, down_sib, down_sum, down_far),
+    ]
+    small_copies = [
+        push(small.at[seqs[k]], small_seq.at[k - 1], m_send.at[0, k], m_recv.at[0, k], (d, seqs[k]))
+        for k in range(1, S)
+    ]
+    order = list(range(1, C)) + [0]
+    near = [
+        {
+            k: push(
+                part.at[2 * chips[k] + 1 - core],
+                sib.at[k],
+                n_send.at[j, k],
+                n_recv.at[j, k],
+                sibling,
+            )
+            for k in order
+        }
+        for j, (part, sib, _, _) in enumerate(items)
+    ]
+    far = []
+    for j, (part, sib, total, away) in enumerate(items):
+        group = []
+        for k in range(1, C):
+            near[j][k].wait_recv()
+            total[k - 1] = (
+                part[2 * chips[k] + core].astype(jnp.float32) + sib[k].astype(jnp.float32)
+            ).astype(jnp.bfloat16)
+            group.append(
+                push(
+                    total.at[k - 1],
+                    away.at[k - 1],
+                    c_send.at[j, k],
+                    c_recv.at[j, k],
+                    (2 * chips[k] + core, s),
+                )
+            )
+        far.append(group)
+
+    for copy in small_copies:
+        copy.wait()
+    row_sum = small[s]
+    for k in range(1, S):
+        row_sum = row_sum + small_seq[k - 1]
+    small_own[...] = row_sum
+    pair = push(small_own, small_sib, m_send.at[1, 0], m_recv.at[1, 0], sibling)
+    pair.wait()
+    small_chip[chip] = small_own[...] + small_sib[...]
+    chip_copies = [
+        push(
+            small_chip.at[chip],
+            small_chip.at[chip],
+            m_send.at[2, k],
+            m_recv.at[2, k],
+            (2 * chips[k] + core, s),
+        )
+        for k in range(1, C)
+    ]
+
+    def finish(j):
+        part, sib, _, away = items[j]
+        near[j][0].wait_recv()
+        total = part[d].astype(jnp.float32) + sib[0].astype(jnp.float32)
+        for k in range(1, C):
+            far[j][k - 1].wait_recv()
+            total = total + away[k - 1].astype(jnp.float32)
+        return total
+
+    seq_part[...] = finish(0).astype(jnp.bfloat16)
+    seq_copies = [
+        push(seq_part.at[seqs[k]], seq_far.at[k - 1], s_send.at[k], s_recv.at[k], (d, seqs[k]))
+        for k in range(1, S)
+    ]
+    for j, out in ((1, o_gate), (2, o_up), (3, o_down)):
+        out[...] = finish(j)
+    for copy in chip_copies:
+        copy.wait()
+    total = small_chip[0]
+    for k in range(1, C):
+        total = total + small_chip[k]
+    o_small[...] = total
+    for copy in seq_copies:
+        copy.wait()
+    total = seq_part[s].astype(jnp.float32)
+    for k in range(1, S):
+        total = total + seq_far[k - 1].astype(jnp.float32)
+    o_attn[...] = total
+    for j in range(4):
+        for k in range(C):
+            near[j][k].wait_send()
+        for copy in far[j]:
+            copy.wait_send()
+
+
+def scatter_all(S, DP, attn, gate, up, down, small):
+    C = DP // 2
+    blocks = [attn.shape[1:], gate.shape[1:], up.shape[1:], down.shape[1:]]
+
+    def low(*shape):
+        return pltpu.VMEM(shape, jnp.bfloat16)
+
+    def wide(*shape):
+        return pltpu.VMEM(shape, jnp.float32)
+
+    def out(*shape):
+        return jax.ShapeDtypeStruct(shape, jnp.float32)
+
+    dma = pltpu.SemaphoreType.DMA
+    return pl.pallas_call(
+        functools.partial(scatter_kernel, S, C),
+        out_shape=[
+            out(*attn.shape[2:]),
+            out(*blocks[1]),
+            out(*blocks[2]),
+            out(*blocks[3]),
+            out(*small.shape[1:]),
+        ],
+        in_specs=[pl.BlockSpec(memory_space=pltpu.VMEM)] * 5,
+        out_specs=[pl.BlockSpec(memory_space=pltpu.VMEM)] * 5,
+        scratch_shapes=[low(C, *block) for block in blocks]
+        + [low(C - 1, *block) for block in blocks]
+        + [low(C - 1, *block) for block in blocks]
+        + [
+            low(S, *attn.shape[2:]),
+            low(S - 1, *attn.shape[2:]),
+            wide(S - 1, *small.shape[1:]),
+            wide(*small.shape[1:]),
+            wide(*small.shape[1:]),
+            wide(C, *small.shape[1:]),
+            dma((4, C)),
+            dma((4, C)),
+            dma((4, C)),
+            dma((4, C)),
+            dma((S,)),
+            dma((S,)),
+            dma((3, max(S, C))),
+            dma((3, max(S, C))),
+        ],
+        compiler_params=pltpu.CompilerParams(
+            collective_id=1, has_side_effects=True, vmem_limit_bytes=VMEM_BYTES
+        ),
+    )(attn, gate, up, down, small)
 
 
 def on_device(
@@ -89,9 +389,9 @@
     def as_row(vector):
         return jnp.pad(vector, (0, pack_cols - vector.shape[0]))[None]
 
-    packed = jnp.concatenate(
+    attn_own = jnp.concatenate([w_query, w_out, w_key, w_value], axis=1)
+    vec_own = jnp.concatenate(
         [
-            jnp.concatenate([w_query, w_out, w_key, w_value], axis=1),
             jnp.concatenate([attn_gain, b_query, b_key, b_value])[None],
             as_row(mlp_gain),
             as_row(segments[0].astype(jnp.bfloat16)),
@@ -99,27 +399,27 @@
         ],
         axis=0,
     )
-    by_seq = lax.all_gather(packed, "seq", axis=0)
-    attn_all = lax.all_gather(by_seq[:, :rows], "dp", axis=0)
+    d_result = cotangent[0]
+    attn_all, by_seq, d_result_all, mat_gate, mat_up, mat_down = gather_all(
+        seq_count, dp_count, attn_own, vec_own, d_result, w_gate, w_up, w_down.T
+    )
+    d_result_all = d_result_all.reshape(full_len, model_width)
+    mat_gate = mat_gate.reshape(model_width, -1)
+    mat_up = mat_up.reshape(model_width, -1)
+    mat_down = mat_down.reshape(model_width, -1)
     attn_all = attn_all.transpose(0, 2, 1, 3).reshape(model_width, seq_count, pack_cols)
     mat_query = attn_all[:, :, :q_cols].reshape(model_width, model_width)
     mat_out = attn_all[:, :, q_cols : 2 * q_cols].reshape(model_width, model_width)
     mat_key = attn_all[:, :, 2 * q_cols : 2 * q_cols + k_cols].reshape(model_width, kv_width)
     mat_value = attn_all[:, :, 2 * q_cols + k_cols :].reshape(model_width, kv_width)
-    vectors = by_seq[:, rows].astype(jnp.float32)
+    vectors = by_seq[:, 0].astype(jnp.float32)
     gain_one = vectors[:, :q_cols].reshape(model_width)
     bias_query = vectors[:, q_cols : 2 * q_cols].reshape(model_width)
     bias_key = vectors[:, 2 * q_cols : 2 * q_cols + k_cols].reshape(kv_width)
     bias_value = vectors[:, 2 * q_cols + k_cols :].reshape(kv_width)
-    gain_two = by_seq[:, rows + 1, :q_cols].astype(jnp.float32).reshape(model_width)
-    seg_all = by_seq[:, rows + 2, :local_len].reshape(full_len)
+    gain_two = by_seq[:, 1, :q_cols].astype(jnp.float32).reshape(model_width)
+    seg_all = by_seq[:, 2, :local_len].reshape(full_len)
     seg_own = segments[0].astype(jnp.bfloat16)
-
-    mat_gate = lax.all_gather(w_gate, "dp", axis=0, tiled=True)
-    mat_up = lax.all_gather(w_up, "dp", axis=0, tiled=True)
-    mat_down = lax.all_gather(w_down.T, "dp", axis=0, tiled=True)
-    d_result = cotangent[0]
-    d_result_all = lax.all_gather(d_result, "seq", axis=0, tiled=True)
 
     own_pos = seq_place * local_len + jnp.arange(local_len, dtype=jnp.int32)
     all_pos = jnp.arange(full_len, dtype=jnp.int32)
@@ -170,12 +470,11 @@
         jnp.float32
     )
     branch_all = contract(hidden, mat_down, 1, 1).astype(jnp.bfloat16)
+    branch_all, d_norm_part = lax.optimization_barrier((branch_all, d_norm_part))
     branch_sum = lax.psum_scatter(branch_all, "seq", scatter_dimension=0, tiled=True)
     output = (residual + branch_sum.astype(jnp.float32)).astype(jnp.bfloat16)[None]
-    grad_gate, grad_up, grad_down = (
-        lax.psum_scatter(
-            contract(left, right, 0, 0).astype(jnp.bfloat16), "dp", scatter_dimension=0, tiled=True
-        ).astype(jnp.float32)
+    part_gate, part_up, part_down = (
+        contract(left, right, 0, 0).astype(jnp.bfloat16).reshape(dp_count, rows, -1)
         for left, right in ((normed_two, d_gate), (normed_two, d_up), (d_result_all, hidden))
     )
 
@@ -235,9 +534,6 @@
         ],
         axis=3,
     ).transpose(0, 2, 1, 3)
-    attn_grads = lax.psum_scatter(attn_grads, "dp", scatter_dimension=0)
-    attn_grads = lax.psum_scatter(attn_grads, "seq", scatter_dimension=0).astype(jnp.float32)
-
     grad_bias_query = jnp.sum(d_query_lin, axis=0, dtype=jnp.float32)
     grad_bias_key = jnp.sum(d_key_lin, axis=0, dtype=jnp.float32)
     grad_bias_value = jnp.sum(d_value_lin, axis=0, dtype=jnp.float32)
@@ -266,8 +562,11 @@
         ],
         axis=1,
     )
-    small = lax.psum(small, ("dp", "seq"))
-    small = lax.dynamic_index_in_dim(small, seq_place, 0, keepdims=False)
+    small = jnp.pad(small[:, None], ((0, 0), (0, 7), (0, -small.shape[1] % 128)))
+    attn_grads, grad_gate, grad_up, grad_down, small = scatter_all(
+        seq_count, dp_count, attn_grads, part_gate, part_up, part_down, small
+    )
+    small = small[0]
     return (
         output,
         d_inputs[None],
@@ -277,7 +576,7 @@
         attn_grads[:, 2 * q_cols : 2 * q_cols + k_cols],
         small[3 * q_cols : 3 * q_cols + k_cols],
         attn_grads[:, 2 * q_cols + k_cols :],
-        small[3 * q_cols + k_cols :],
+        small[3 * q_cols + k_cols : 3 * q_cols + 2 * k_cols],
         attn_grads[:, q_cols : 2 * q_cols],
         small[2 * q_cols : 3 * q_cols],
         grad_gate,

time: 685 us -> 453 us (0.66)
  waiting for transfers between devices: 364 us -> 80.4 us
  Pallas kernels: 0 us -> 137 us
  blocking collectives: 73 us -> 16.5 us
  matrix products: 123 us -> 100 us
    pallas_call x0 -> x2, Pallas kernels: none -> 137 us  [the longest x1 69.5 us: scatter_all(): pl.pallas_call(functools.partial(scatter_kernel, S, C), out_shape=[out(*a...]
    reduce_scatter x4 -> x0, waiting for transfers between devices: 129 us -> none  [the longest x2 83.3 us: on_device(): lax.psum_scatter(contract(left, right, 0, 0).astype(jnp.bfloat16), 'dp',...]
    all_gather x5 -> x0, waiting for transfers between devices: 120 us -> none  [the longest x1 35.7 us: on_device(): d_result_all = lax.all_gather(d_result, 'seq', axis=0, tiled=True)]
    psum x1 -> x0, blocking collectives: 39.6 us -> none  [on_device(): small = lax.psum(small, ('dp', 'seq'))]
    reduce_scatter x1, waiting for transfers between devices: 39.6 us -> 7.2 us  [on_device(): lax.psum_scatter(branch_all, 'seq', scatter_dimension=0, tiled=True)]
    all_gather x1 -> x0, blocking collectives: 17.4 us -> none  [on_device(): by_seq = lax.all_gather(packed, 'seq', axis=0)]
    convert_element_type x1 -> x4, local copies, waits for them, and re-layouts: 0.08 us -> 13.4 us  [the longest x3 12.7 us: on_device(): contract(left, right, 0, 0).astype(jnp.bfloat16).reshape(dp_count, rows, -1)]
    dot_general x14, matrix products: 53 us -> 44.2 us  [contract(): lax.dot_general(left_mat, right_mat, (((left_dim,), (right_dim,)), ((), (...]
  transfers between devices with their start and end apart: 14 -> 4, of which waited for: 10 -> 4; matrix products, arithmetic and copies ran while one was open for 22% -> 13% of each run, Pallas kernels for 0% -> 0%
where the time goes in v2:
time: 453 us; the launch traced here: 448 us
  Pallas kernels  137 us (30%)
  matrix products  100 us (22%)
  waiting for transfers between devices  80.4 us (18%)
  local copies, waits for them, and re-layouts  61.5 us (14%)
  other arithmetic  37.1 us (8%)
  blocking collectives  16.5 us (4%)
  between operations  14.8 us (3%)
    pallas_call x1, Pallas kernels, scatter_all(): pl.pallas_call(functools.partial(scatter_kernel, S, C), out_shape=[out(*a...  69.5 us
    pallas_call x1, Pallas kernels, gather_all(): pl.pallas_call(functools.partial(gather_kernel, S, C), out_shape=[out(DP,...  67.1 us
    dot_general x14, matrix products, contract(): lax.dot_general(left_mat, right_mat, (((left_dim,), (right_dim,)), ((), (...  44.2 us
    all_gather x1, waiting for transfers between devices, on_device(): normed_two = lax.all_gather(normed_loc, 'seq', axis=0, tiled=True)  39.4 us
    reduce_scatter x1, waiting for transfers between devices, on_device(): lax.psum_scatter(d_norm_all, 'seq', scatter_dimension=0, tiled=True)  31.7 us
    reshape x8, local copies, waits for them, and re-layouts, on_device(): item.astype(jnp.bfloat16).reshape(dp_count, rows, seq_count, -1)  17.3 us
    all_gather x1, blocking collectives, on_device(): kv_all = lax.all_gather(kv_loc, 'seq', axis=0, tiled=True)  16.5 us
    convert_element_type x3, local copies, waits for them, and re-layouts, on_device(): contract(left, right, 0, 0).astype(jnp.bfloat16).reshape(dp_count, rows, -1)  12.7 us
  transfers between devices with their start and end apart: 4, of which 4 were waited for; matrix products, arithmetic and copies ran while one was open for 13% of the time, Pallas kernels for 0%

profile of v2, /device:TPU:0, one launch (start us, length us, event | category | flops | bytes accessed | tf_op | source)
XLA Modules:
  0.0 447.7 jit_solution(17896096248105944131)
XLA Ops:
  14.0 67.1 %shard_map.254 = (bf16[8,4,112,512]{3,2,1,0:T(8,128)(2,1)}, bf16[4,16,512]{2,1,0:T(8,128)(2,1)}, bf16[4,256,896]{2,1,0:T(8,128)(2,1)}, bf16[8,112,1216]{2,1,0:T(...) custom-call(bf16[112,512]{1,0:T(8,128)(2,1)} %pad_maximum_fusion.6.attn, ...), custom_call_target="tpu_custom_call" | custom-call | tf_op jit(solution)/shard_map/pallas_call | solution.py:169
  96.8 16.5 %all_gather.6 = bf16[1024,256]{0,1:T(8,128)(2,1)S(1)} all-gather(bf16[256,256]{0,1:T(8,128)(2,1)S(1)} %pad_maximum_fusion.5), channel_id=1, replica_groups=mesh['dp'=8,'seq'=4] {'seq'}, dimensions={0}, use_global_device_ids=true | all-gather | bytes 655360 | tf_op jit(solution)/shard_map/all_gather | solution.py:440
  123.0 6.5 %fusion.62 = (f32[2,7,256]{2,1,0:T(8,128)S(1)}, f32[2,7,256,1024]{2,3,1,0:T(8,128)}) fusion(bf16[1024,2,64,1]{0,2,3,1:T(8,128)(2,1)S(1)} %bitcast.192, bf16[256,2,7,32]{0,3,2,1:T(8,128)(2,1)S(1)} %bitcast.196, bf16[256,2,7,32]{0,3,2,1:T(8,128)(2,1)S(1)} %bitcast.194, pred[256,1024]{0,1:T(8,128)(4,1)S(1)} %fusion.25), kind=kOutput, calls=%fused_computation.127 | convolution fusion | flops 481686016 | bytes 15677440 | tf_op jit(solution)/shard_map/qgjd,kgd->gjqk/dot_general | solution.py:57
  129.5 7.1 %fusion.3 = f32[2,7,256]{2,1,0:T(8,128)S(1)} fusion(f32[2,7,256,1024]{2,3,1,0:T(8,128)} %get-tuple-element.111, f32[2,7,256]{2,1,0:T(8,128)S(1)} %get-tuple-element.110), kind=kLoop, calls=%fused_computation.9 | loop fusion | flops 7336448 | bytes 14708736 | tf_op jit(solution)/shard_map/reduce_sum | solution.py:446
  136.6 6.6 %fusion.10 = bf16[2,64,7,256]{3,1,2,0:T(8,128)(2,1)S(1)} fusion(bf16[1024,2,64,1]{0,2,3,1:T(8,128)(2,1)S(1)} %bitcast.201, f32[2,7,256,1024]{2,3,1,0:T(8,128)} %get-tuple-element.111, f32[2,7,256]{2,1,0:T(8,128)S(1)} %fusion.3, f32[2,7,256]{2,1,0:T(8,128)S(1)} %get-tuple-element.110), kind=kOutput, calls=%fused_computation.33 | convolution fusion | flops 481001472 | bytes 15429632 | tf_op jit(solution)/shard_map/gjqk,kgd->qgjd/dot_general | solution.py:449
  145.7 39.4 %all-gather.2.cloned.1.call-done = bf16[1024,896]{1,0:T(8,128)(2,1)} async-done(((bf16[256,896]{1,0:T(8,128)(2,1)}), bf16[1024,896]{1,0:T(8,128)(2,1)}) %all-gather.2.cloned.1.call-update) | async-done | bytes 1835024 | tf_op jit(solution)/shard_map/all_gather | solution.py:455
  185.1 5.2 %fusion.64 = f32[1024,1216]{0,1:T(8,128)S(1)} fusion(bf16[1024,896]{1,0:T(8,128)(2,1)} %all-gather.2.cloned.1.call-done, bf16[896,1216]{1,0:T(8,128)(2,1)} %bitcast.225), kind=kOutput, calls=%fused_computation.129 | convolution fusion | flops 2231369728 | bytes 8994816 | tf_op jit(solution)/shard_map/dot_general | solution.py:457
  193.3 7.0 %multiply_convert_fusion = (bf16[1024,1216]{0,1:T(8,128)(2,1)}, bf16[1024,1216]{0,1:T(8,128)(2,1)}, bf16[1024,1216]{0,1:T(8,128)(2,1)}) fusion(f32[1024,1216]{0,1:T(8,128)S(1)} %fusion.63, f32[1024,1216]{0,1:T(8,128)S(1)} %fusion.64, bf16[1024,896]{1,0:T(8,128)(2,1)S(1)} %bitcast.230, bf16[896,1216]{1,0:T(8,128)(2,1)S(1)} %bitcast.224), kind=kOutput, calls=%fused_computation.14 | convolution fusion | flops 2248802304 | bytes 21446656 | tf_op jit(solution)/shard_map/dot_general | solution.py:458
  200.3 4.8 %fusion.65 = f32[1024,896]{1,0:T(8,128)S(1)} fusion(bf16[1024,1216]{0,1:T(8,128)(2,1)} %get-tuple-element.73, bf16[896,1216]{1,0:T(8,128)(2,1)S(1)} %bitcast.228), kind=kOutput, calls=%fused_computation.130 | convolution fusion | flops 2231369728 | bytes 8339456 | tf_op jit(solution)/shard_map/dot_general | solution.py:20
  205.1 4.2 add_convert_fusion
  209.3 6.7 %convolution_convert_fusion.3 = bf16[1024,896]{1,0:T(8,128)(2,1)} fusion(bf16[1024,1216]{0,1:T(8,128)(2,1)} %get-tuple-element.74, bf16[896,1216]{1,0:T(8,128)(2,1)} %bitcast.223), kind=kOutput, calls=%fused_computation.24 | convolution fusion | flops 2232287232 | bytes 6504448 | tf_op jit(solution)/shard_map/dot_general | solution.py:20
  216.0 31.7 %reduce-scatter.4.cloned.1.call-done = bf16[256,896]{1,0:T(8,128)(2,1)} async-done(((bf16[1024,896]{1,0:T(8,128)(2,1)}), bf16[256,896]{1,0:T(8,128)(2,1)}) %reduce-scatter.4.cloned.1.call-update) | async-done | bytes 458768 | tf_op jit(solution)/shard_map/reduce_scatter | solution.py:469
  248.9 6.6 %convolution_convert_fusion = bf16[896,1216]{0,1:T(8,128)(2,1)} fusion(bf16[1024,1216]{0,1:T(8,128)(2,1)} %get-tuple-element.74, bf16[1024,896]{1,0:T(8,128)(2,1)} %bitcast.229), kind=kOutput, calls=%fused_computation.21 | convolution fusion | flops 2232459264 | bytes 6504448 | tf_op jit(solution)/shard_map/dot_general | solution.py:20
  255.5 4.4 copy.71
  259.9 6.4 %convolution_convert_fusion.2 = bf16[896,1216]{0,1:T(8,128)(2,1)} fusion(bf16[1024,1216]{0,1:T(8,128)(2,1)} %get-tuple-element.73, bf16[1024,896]{1,0:T(8,128)(2,1)} %all-gather.2.cloned.1.call-done), kind=kOutput, calls=%fused_computation.23 | convolution fusion | flops 2232459264 | bytes 6504448 | tf_op jit(solution)/shard_map/dot_general | solution.py:20
  266.3 4.2 copy.69
  270.5 6.4 %convolution_convert_fusion.1 = bf16[896,1216]{0,1:T(8,128)(2,1)} fusion(bf16[1024,1216]{0,1:T(8,128)(2,1)} %get-tuple-element.72, bf16[1024,896]{1,0:T(8,128)(2,1)} %all-gather.2.cloned.1.call-done), kind=kOutput, calls=%fused_computation.22 | convolution fusion | flops 2232459264 | bytes 6504448 | tf_op jit(solution)/shard_map/dot_general | solution.py:20
  281.4 7.2 %reduce-scatter.6.cloned.1.call-done = bf16[256,896]{1,0:T(8,128)(2,1)} async-done(((bf16[1024,896]{1,0:T(8,128)(2,1)}), bf16[256,896]{1,0:T(8,128)(2,1)}) %reduce-scatter.6.cloned.1.call-update) | async-done | bytes 458768 | tf_op jit(solution)/shard_map/reduce_scatter | solution.py:474
  292.1 7.7 %fusion.16 = bf16[2,64,1024]{2,1,0:T(8,128)(2,1)S(1)} fusion(bf16[256,2,7,64]{0,3,2,1:T(8,128)(2,1)S(1)} %bitcast.185, f32[2,7,256,1024]{2,3,1,0:T(8,128)} %get-tuple-element.111, f32[2,7,256]{2,1,0:T(8,128)S(1)} %log_add_fusion), kind=kOutput, calls=%fused_computation.38 | convolution fusion | flops 477233152 | bytes 15415296 | tf_op jit(solution)/shard_map/gjqk,qgjd->kgd/dot_general | solution.py:499
  299.8 10.9 %fusion = (f32[2,7,256]{2,1,0:T(8,128)S(1)}, f32[2,1024,256,7]{2,1,3,0:T(8,128)}) fusion(f32[2,7,256,1024]{2,3,1,0:T(8,128)} %get-tuple-element.111, f32[2,7,256]{2,1,0:T(8,128)S(1)} %log_add_fusion, bf16[1024,2,64,1]{0,2,3,1:T(8,128)(2,1)S(1)} %bitcast.202, bf16[256,2,7,64]{0,3,2,1:T(8,128)(2,1)S(1)} %bitcast.186), kind=kOutput, calls=%fused_computation.2 | convolution fusion | flops 480768512 | bytes 30109696 | tf_op jit(solution)/shard_map/qgjd,kgd->gjqk/dot_general | solution.py:498
  310.7 7.6 %fusion.2 = bf16[2,7,256,1024]{2,3,1,0:T(8,128)(2,1)S(1)} fusion(f32[2,1024,256,7]{2,1,3,0:T(8,128)} %get-tuple-element.115, f32[2,7,256,1024]{2,3,1,0:T(8,128)S(1)} %bitcast.175, f32[2,7,256]{2,1,0:T(8,128)S(1)} %get-tuple-element.114, f32[2,7,256]{2,1,0:T(8,128)S(1)} %log_add_fusion), kind=kLoop, calls=%fused_computation.4 | loop fusion | flops 14680064 | bytes 36728832 | tf_op jit(solution)/shard_map/convert_element_type | solution.py:504
  332.6 5.3 %reshape.408 = bf16[8,112,4,224]{3,2,1,0:T(4,128)(2,1)} reshape(bf16[896,896]{1,0:T(8,128)(2,1)} %convolution_convert_fusion.5) | data formatting | bytes 3211264 | tf_op jit(solution)/shard_map/reshape | solution.py:532
  354.7 6.2 %maximum_bitcast_fusion.attn = bf16[8,4,112,512]{3,2,1,0:T(8,128)(2,1)} fusion(bf16[8,112,4,32]{3,1,2,0:T(8,128)(2,1)S(1)} %copy.68, bf16[8,112,4,32]{3,1,2,0:T(8,128)(2,1)S(1)} %copy.67, bf16[8,112,4,224]{3,1,2,0:T(8,128)(2,1)} %copy.66, bf16[8,112,4,224]{3,1,2,0:T(8,128)(2,1)} %copy.65), kind=kLoop, calls=%fused_computation.18 | loop fusion | flops 14680064 | bytes 7340032 | tf_op jit(solution)/shard_map/transpose | solution.py:536
  360.9 69.5 %shard_map.255 = (f32[112,512]{1,0:T(8,128)}, f32[112,1216]{1,0:T(8,128)}, f32[112,1216]{1,0:T(8,128)}, f32[112,1216]{1,0:T(8,128)}, f32[8,768]{1,0:T(8,128)}) custom-call(bf16[8,4,112,512]{3,2,1,0:T(8,128)(2,1)} %maximum_bitcast_fusion.attn, bf16[8,112,1216]{2,1,0:T(8,128)(2,1)} %bitcast.181, bf16[8,112,1216]{2,1,0:T(8,128)(2,1)} %bitcast.182, ...), custom_call_target="tpu_custom_call" | custom-call | tf_op jit(solution)/shard_map/pallas_call | solution.py:323
  (211 shorter events, 87.7 us)
Async XLA Ops:
  7.2 178.0 %all-gather.2.cloned.1.call-start = ((), (), s32[]{:S(2)}) async-start(), calls=%async_computation.3 | async-start | bytes 2293760 | tf_op jit(solution)/shard_map/all_gather | solution.py:455
  90.0 27.1 %copy-start.31 = (f32[256]{0:T(256)}, f32[256]{0:T(256)S(1)}, u32[]{:S(2)}) copy-start(f32[256]{0:T(256)S(1)} %get-tuple-element.107) | copy-start | bytes 3076
  91.5 25.6 %copy-start.29 = (f32[896]{0:T(1024)}, f32[896]{0:T(1024)S(1)}, u32[]{:S(2)}) copy-start(f32[896]{0:T(1024)S(1)} %mul.321) | copy-start | bytes 10756
  113.4 9.6 %copy-start.5 = (bf16[1024,128]{0,1:T(8,128)(2,1)}, bf16[1024,128]{0,1:T(8,128)(2,1)S(1)}, u32[]{:S(2)}) copy-start(bf16[1024,128]{0,1:T(8,128)(2,1)S(1)} %get-tuple-element.85) | copy-start | bytes 786436
  113.4 23.2 %copy-start.12 = (bf16[1024,128]{0,1:T(8,128)(2,1)}, bf16[1024,128]{0,1:T(8,128)(2,1)S(1)}, u32[]{:S(2)}) copy-start(bf16[1024,128]{0,1:T(8,128)(2,1)S(1)} %get-tuple-element.86) | copy-start | bytes 786436
  122.7 6.8 %copy-start.7 = (bf16[256,14,32]{0,2,1:T(8,128)(2,1)}, bf16[256,14,32]{0,2,1:T(8,128)(2,1)S(1)}, u32[]{:S(2)}) copy-start(bf16[256,14,32]{0,2,1:T(8,128)(2,1)S(1)} %get-tuple-element.81) | copy-start | bytes 688132
  122.7 6.8 %copy-start.9 = (bf16[256,14,32]{0,2,1:T(8,128)(2,1)}, bf16[256,14,32]{0,2,1:T(8,128)(2,1)S(1)}, u32[]{:S(2)}) copy-start(bf16[256,14,32]{0,2,1:T(8,128)(2,1)S(1)} %get-tuple-element.82) | copy-start | bytes 688132
  136.6 6.7 %copy-start.27 = (f32[2,7,256]{2,1,0:T(8,128)}, f32[2,7,256]{2,1,0:T(8,128)S(1)}, u32[]{:S(2)}) copy-start(f32[2,7,256]{2,1,0:T(8,128)S(1)} %fusion.3) | copy-start | bytes 43012
  145.1 102.6 %reduce-scatter.4.cloned.1.call-start = ((), (), s32[]{:S(2)}) async-start(), calls=%async_computation.4 | async-start | bytes 2293760 | tf_op jit(solution)/shard_map/reduce_scatter | solution.py:469
  185.1 5.2 %copy-start.41 = (bf16[1024,896]{1,0:T(8,128)(2,1)S(1)}, bf16[1024,896]{1,0:T(8,128)(2,1)}, u32[]{:S(2)}) copy-start(bf16[1024,896]{1,0:T(8,128)(2,1)} %all-gather.2.cloned.1.call-done) | copy-start | bytes 5505028
  209.3 79.3 %reduce-scatter.6.cloned.1.call-start = ((), (), s32[]{:S(2)}) async-start(), calls=%async_computation.5 | async-start | bytes 2293760 | tf_op jit(solution)/shard_map/reduce_scatter | solution.py:474
  216.0 32.9 %copy-start.28 = (f32[2,7,256]{2,1,0:T(8,128)S(1)}, f32[2,7,256]{2,1,0:T(8,128)}, u32[]{:S(2)}) copy-start(f32[2,7,256]{2,1,0:T(8,128)} %copy-done.27) | copy-start | bytes 43012
  248.8 32.2 %copy-start.2 = (f32[256,896]{1,0:T(8,128)}, f32[256,896]{1,0:T(8,128)S(1)}, u32[]{:S(2)}) copy-start(f32[256,896]{1,0:T(8,128)S(1)} %convert_element_type.215) | copy-start | bytes 2752516
  248.8 95.0 %reduce-scatter.8.cloned.1.call-start = ((), (), s32[]{:S(2)}) async-start(), calls=%async_computation.6 | async-start | bytes 655360 | tf_op jit(solution)/shard_map/reduce_scatter | solution.py:512
  292.0 7.7 %copy-start.13 = (bf16[1024,128]{0,1:T(8,128)(2,1)S(1)}, bf16[1024,128]{0,1:T(8,128)(2,1)}, u32[]{:S(2)}) copy-start(bf16[1024,128]{0,1:T(8,128)(2,1)} %copy-done.12) | copy-start | bytes 786436
  292.0 18.6 %slice-start = ((s8[14680064]{0:T(1024)(128)(4,1)}), s8[4194304]{0:T(1024)(128)(4,1)S(1)}, s32[]{:S(2)}) async-start(s8[14680064]{0:T(1024)(128)(4,1)} %bitcast.174), calls=%async_computation.7 | async-start | bytes 8388608
  292.1 18.6 %slice-start.1 = ((s8[14680064]{0:T(1024)(128)(4,1)}), s8[4194304]{0:T(1024)(128)(4,1)S(1)}, s32[]{:S(2)}) async-start(s8[14680064]{0:T(1024)(128)(4,1)} %bitcast.174), calls=%async_computation.8 | async-start | bytes 8388608
  299.7 10.9 %slice-start.2 = ((s8[14680064]{0:T(1024)(128)(4,1)}), s8[4194304]{0:T(1024)(128)(4,1)S(1)}, s32[]{:S(2)}) async-start(s8[14680064]{0:T(1024)(128)(4,1)} %bitcast.174), calls=%async_computation.9 | async-start | bytes 8388608
  299.8 10.9 %slice-start.3 = ((s8[14680064]{0:T(1024)(128)(4,1)}), s8[2097152]{0:T(1024)(128)(4,1)S(1)}, s32[]{:S(2)}) async-start(s8[14680064]{0:T(1024)(128)(4,1)} %bitcast.174), calls=%async_computation.10 | async-start | bytes 4194304
  310.7 7.6 %copy-start.8 = (bf16[256,14,32]{0,2,1:T(8,128)(2,1)S(1)}, bf16[256,14,32]{0,2,1:T(8,128)(2,1)}, u32[]{:S(2)}) copy-start(bf16[256,14,32]{0,2,1:T(8,128)(2,1)} %copy-done.7) | copy-start | bytes 688132
  310.7 7.6 %copy-start.10 = (bf16[256,14,32]{0,2,1:T(8,128)(2,1)S(1)}, bf16[256,14,32]{0,2,1:T(8,128)(2,1)}, u32[]{:S(2)}) copy-start(bf16[256,14,32]{0,2,1:T(8,128)(2,1)} %copy-done.9) | copy-start | bytes 688132
  341.9 6.5 %copy-start.15 = (bf16[896,4,32]{0,2,1:T(8,128)(2,1)S(1)}, bf16[896,4,32]{0,2,1:T(8,128)(2,1)}, u32[]{:S(2)}) copy-start(bf16[896,4,32]{0,2,1:T(8,128)(2,1)} %copy-done.14) | copy-start | bytes 688132
  360.9 76.5 %copy-start.4 = (f32[256,896]{1,0:T(8,128)S(1)}, f32[256,896]{1,0:T(8,128)}, u32[]{:S(2)}) copy-start(f32[256,896]{1,0:T(8,128)} %get-tuple-element.116) | copy-start | bytes 2752516
  360.9 76.4 %copy-start.33 = (f32[256]{0:T(256)S(1)}, f32[256]{0:T(256)}, u32[]{:S(2)}) copy-start(f32[256]{0:T(256)} %get-tuple-element.106) | copy-start | bytes 3076
  (27 other events, 77.0 us)
Sparse Core Ops, SparseCore 0:
  145.2 39.9 all-gather.1
  209.4 38.2 reduce-scatter.3
  250.0 38.5 reduce-scatter.5
  323.0 20.7 reduce-scatter.7

commit v3 on v2

--- a/solution.py
+++ b/solution.py
@@ -407,11 +407,23 @@
     mat_gate = mat_gate.reshape(model_width, -1)
     mat_up = mat_up.reshape(model_width, -1)
     mat_down = mat_down.reshape(model_width, -1)
-    attn_all = attn_all.transpose(0, 2, 1, 3).reshape(model_width, seq_count, pack_cols)
-    mat_query = attn_all[:, :, :q_cols].reshape(model_width, model_width)
-    mat_out = attn_all[:, :, q_cols : 2 * q_cols].reshape(model_width, model_width)
-    mat_key = attn_all[:, :, 2 * q_cols : 2 * q_cols + k_cols].reshape(model_width, kv_width)
-    mat_value = attn_all[:, :, 2 * q_cols + k_cols :].reshape(model_width, kv_width)
+    mat_attn = attn_all.transpose(0, 2, 1, 3).reshape(model_width, seq_count * pack_cols)
+
+    def take(field, start, size):
+        field = field.reshape(field.shape[0], seq_count, pack_cols)
+        return field[:, :, start : start + size].reshape(field.shape[0], -1)
+
+    def lay(query=None, out=None, key=None, value=None):
+        def block(item, size):
+            if item is None:
+                return jnp.zeros((local_len, seq_count, size), jnp.bfloat16)
+            return item.reshape(local_len, seq_count, size)
+
+        return jnp.concatenate(
+            [block(query, q_cols), block(out, q_cols), block(key, k_cols), block(value, k_cols)],
+            axis=2,
+        ).reshape(local_len, seq_count * pack_cols)
+
     vectors = by_seq[:, 0].astype(jnp.float32)
     gain_one = vectors[:, :q_cols].reshape(model_width)
     bias_query = vectors[:, q_cols : 2 * q_cols].reshape(model_width)
@@ -427,9 +439,10 @@
     inputs = tokens[0].astype(jnp.float32)
     scale_one = lax.rsqrt(jnp.mean(inputs * inputs, axis=-1, keepdims=True) + norm_eps)
     normed = (inputs * scale_one * gain_one).astype(jnp.bfloat16)
-    query_lin = jnp.dot(normed, mat_query, preferred_element_type=jnp.float32) + bias_query
-    key_lin = jnp.dot(normed, mat_key, preferred_element_type=jnp.float32) + bias_key
-    value_lin = jnp.dot(normed, mat_value, preferred_element_type=jnp.float32) + bias_value
+    lin = jnp.dot(normed, mat_attn, preferred_element_type=jnp.float32)
+    query_lin = take(lin, 0, q_cols) + bias_query
+    key_lin = take(lin, 2 * q_cols, k_cols) + bias_key
+    value_lin = take(lin, 2 * q_cols + k_cols, k_cols) + bias_value
     query_rot = rotate(query_lin.reshape(local_len, H, HD), cosine, sine_table).astype(
         jnp.bfloat16
     )
@@ -448,7 +461,9 @@
     log_total = highest + jnp.log(totals)
     mixed = jnp.einsum("gjqk,kgd->qgjd", prob_low, value_all, preferred_element_type=jnp.float32)
     mixed = mixed.astype(jnp.bfloat16).reshape(local_len, model_width)
-    residual = inputs + jnp.dot(mixed, mat_out, preferred_element_type=jnp.float32)
+    residual = inputs + take(
+        jnp.dot(mixed, mat_attn, preferred_element_type=jnp.float32), q_cols, q_cols
+    )
     scale_two = lax.rsqrt(jnp.mean(residual * residual, axis=-1, keepdims=True) + norm_eps)
     normed_loc = (residual * scale_two * gain_two).astype(jnp.bfloat16)
 
@@ -466,17 +481,19 @@
     d_norm_all = (contract(d_gate, mat_gate, 1, 1) + contract(d_up, mat_up, 1, 1)).astype(
         jnp.bfloat16
     )
-    d_norm_part = lax.psum_scatter(d_norm_all, "seq", scatter_dimension=0, tiled=True).astype(
-        jnp.float32
-    )
+    d_norm_part = lax.psum_scatter(d_norm_all, "seq", scatter_dimension=0, tiled=True)
     branch_all = contract(hidden, mat_down, 1, 1).astype(jnp.bfloat16)
-    branch_all, d_norm_part = lax.optimization_barrier((branch_all, d_norm_part))
-    branch_sum = lax.psum_scatter(branch_all, "seq", scatter_dimension=0, tiled=True)
-    output = (residual + branch_sum.astype(jnp.float32)).astype(jnp.bfloat16)[None]
     part_gate, part_up, part_down = (
         contract(left, right, 0, 0).astype(jnp.bfloat16).reshape(dp_count, rows, -1)
         for left, right in ((normed_two, d_gate), (normed_two, d_up), (d_result_all, hidden))
     )
+
+    d_norm_part, branch_all, part_gate, part_up, part_down = lax.optimization_barrier(
+        (d_norm_part, branch_all, part_gate, part_up, part_down)
+    )
+    d_norm_part = d_norm_part.astype(jnp.float32)
+    branch_sum = lax.psum_scatter(branch_all, "seq", scatter_dimension=0, tiled=True)
+    output = (residual + branch_sum.astype(jnp.float32)).astype(jnp.bfloat16)[None]
 
     grad_gain_two = jnp.sum(d_norm_part * residual * scale_two, axis=0)
     d_scaled_two = d_norm_part * gain_two
@@ -486,9 +503,9 @@
         - residual * scale_two**3 * jnp.mean(d_scaled_two * residual, axis=-1, keepdims=True)
     )
     d_attn = d_residual.astype(jnp.bfloat16)
-    grad_out = contract(mixed, d_attn, 0, 0)
+    d_attn_laid = lay(out=d_attn)
     d_mixed = (
-        contract(d_attn, mat_out, 1, 1)
+        contract(d_attn_laid, mat_attn, 1, 1)
         .astype(jnp.bfloat16)
         .reshape(local_len, KVH, group_size, HD)
     )
@@ -523,25 +540,21 @@
         unrotate(d_key_loc, cosine, sine_table).astype(jnp.bfloat16).reshape(local_len, kv_width)
     )
     d_value_lin = d_kv_loc[:, kv_width:]
-    grad_query = contract(normed, d_query_lin, 0, 0)
-    grad_key = contract(normed, d_key_lin, 0, 0)
-    grad_value = contract(normed, d_value_lin, 0, 0)
-
-    attn_grads = jnp.concatenate(
-        [
-            item.astype(jnp.bfloat16).reshape(dp_count, rows, seq_count, -1)
-            for item in (grad_query, grad_out, grad_key, grad_value)
-        ],
-        axis=3,
-    ).transpose(0, 2, 1, 3)
+    d_lin_laid = lay(query=d_query_lin, key=d_key_lin, value=d_value_lin)
+
+    attn_grads = contract(
+        jnp.concatenate([normed, mixed], axis=0),
+        jnp.concatenate([d_lin_laid, d_attn_laid], axis=0),
+        0,
+        0,
+    )
+    attn_grads = attn_grads.astype(jnp.bfloat16).reshape(dp_count, rows, seq_count, pack_cols)
+    attn_grads = attn_grads.transpose(0, 2, 1, 3)
+
     grad_bias_query = jnp.sum(d_query_lin, axis=0, dtype=jnp.float32)
     grad_bias_key = jnp.sum(d_key_lin, axis=0, dtype=jnp.float32)
     grad_bias_value = jnp.sum(d_value_lin, axis=0, dtype=jnp.float32)
-    d_normed = (
-        contract(d_query_lin, mat_query, 1, 1)
-        + contract(d_key_lin, mat_key, 1, 1)
-        + contract(d_value_lin, mat_value, 1, 1)
-    )
+    d_normed = contract(d_lin_laid, mat_attn, 1, 1)
     grad_gain_one = jnp.sum(d_normed * inputs * scale_one, axis=0)
     d_scaled = d_normed * gain_one
     d_inputs = (

time: 453 us -> 427 us (0.943)
  waiting for transfers between devices: 80.4 us -> 55.1 us
  matrix products: 100 us -> 106 us
    reduce_scatter x1, waiting for transfers between devices: 31.7 us -> 7.58 us  [on_device(): lax.psum_scatter(d_norm_all, 'seq', scatter_dimension=0, tiled=True)]
    reduce_scatter x1, waiting for transfers between devices: 1.98 us -> 14.4 us  [on_device(): lax.psum_scatter(d_kv_full, 'seq', scatter_dimension=0, tiled=True)]
    slice x6 -> x5, local copies, waits for them, and re-layouts: 10.7 us -> 3.17 us  [take(): return field[:, :, start:start + size].reshape(field.shape[0], -1)]
    reduce_scatter x1, waiting for transfers between devices: 7.2 us -> 0.01 us  [on_device(): lax.psum_scatter(branch_all, 'seq', scatter_dimension=0, tiled=True)]
    all_gather x1, waiting for transfers between devices: 39.4 us -> 32.8 us  [on_device(): normed_two = lax.all_gather(normed_loc, 'seq', axis=0, tiled=True)]
    transpose x1 -> x0, other arithmetic: 6.17 us -> none  [on_device(): attn_grads = jnp.concatenate([item.astype(jnp.bfloat16).reshape(dp_count,...]
    dot_general x0 -> x1, local copies, waits for them, and re-layouts: none -> 6.09 us  [on_device(): lin = jnp.dot(normed, mat_attn, preferred_element_type=jnp.float32)]
    convert_element_type x3, local copies, waits for them, and re-layouts: 12.7 us -> 7.79 us  [on_device(): contract(left, right, 0, 0).astype(jnp.bfloat16).reshape(dp_count, rows, -1)]
  transfers between devices with their start and end apart: 4 -> 4, of which waited for: 4 -> 3; matrix products, arithmetic and copies ran while one was open for 13% -> 18% of each run, Pallas kernels for 0% -> 17%
where the time goes in v3:
time: 427 us; the launch traced here: 419 us
  Pallas kernels  136 us (32%)
  matrix products  106 us (25%)
  local copies, waits for them, and re-layouts  57.2 us (13%)
  waiting for transfers between devices  55.1 us (13%)
  other arithmetic  32.7 us (8%)
  blocking collectives  16.3 us (4%)
  between operations  14.8 us (3%)
    pallas_call x1, Pallas kernels, scatter_all(): pl.pallas_call(functools.partial(scatter_kernel, S, C), out_shape=[out(*a...  69.3 us
    pallas_call x1, Pallas kernels, gather_all(): pl.pallas_call(functools.partial(gather_kernel, S, C), out_shape=[out(DP,...  67.1 us
    dot_general x9, matrix products, contract(): lax.dot_general(left_mat, right_mat, (((left_dim,), (right_dim,)), ((), (...  42.3 us
    all_gather x1, waiting for transfers between devices, on_device(): normed_two = lax.all_gather(normed_loc, 'seq', axis=0, tiled=True)  32.8 us
    all_gather x1, blocking collectives, on_device(): kv_all = lax.all_gather(kv_loc, 'seq', axis=0, tiled=True)  16.3 us
    reduce_scatter x1, waiting for transfers between devices, on_device(): lax.psum_scatter(d_kv_full, 'seq', scatter_dimension=0, tiled=True)  14.4 us
    reshape x2, local copies, waits for them, and re-layouts, on_device(): attn_grads.astype(jnp.bfloat16)  12 us
    dot_general x1, matrix products, on_device(): jnp.einsum('qgjd,kgd->gjqk', d_mixed, value_all, preferred_element_type=j...  10.9 us
  transfers between devices with their start and end apart: 4, of which 3 were waited for; matrix products, arithmetic and copies ran while one was open for 18% of the time, Pallas kernels for 17%

profile of v3, /device:TPU:0, one launch (start us, length us, event | category | flops | bytes accessed | tf_op | source)
XLA Modules:
  0.0 418.8 jit_solution(11273957346160104374)
XLA Ops:
  15.8 67.1 %shard_map.254 = (bf16[8,4,112,512]{3,2,1,0:T(8,128)(2,1)}, bf16[4,16,512]{2,1,0:T(8,128)(2,1)}, bf16[4,256,896]{2,1,0:T(8,128)(2,1)}, bf16[8,112,1216]{2,1,0:T(...) custom-call(bf16[112,512]{1,0:T(8,128)(2,1)} %pad_maximum_fusion.6.attn, ...), custom_call_target="tpu_custom_call" | custom-call | tf_op jit(solution)/shard_map/pallas_call | solution.py:169
  86.0 4.9 %copy.54 = bf16[8,112,4,512]{3,2,1,0:T(4,128)(2,1)S(1)} copy(bf16[8,112,4,512]{3,1,2,0:T(8,128)(2,1)} %bitcast.201) | data formatting | bytes 7340032 | tf_op jit(solution)/shard_map/transpose | solution.py:410
  93.9 6.1 %copy.86 = bf16[2048,896]{1,0:T(8,128)(2,1)} copy(bf16[2048,896]{0,1:T(8,128)(2,1)} %bitcast.189) | data formatting | bytes 7340032 | tf_op jit(solution)/shard_map/dot_general | solution.py:442
  107.7 16.3 %all_gather.6 = bf16[1024,256]{0,1:T(8,128)(2,1)S(1)} all-gather(bf16[256,256]{0,1:T(8,128)(2,1)S(1)} %pad_maximum_fusion.5), channel_id=1, replica_groups=mesh['dp'=8,'seq'=4] {'seq'}, dimensions={0}, use_global_device_ids=true | all-gather | bytes 655360 | tf_op jit(solution)/shard_map/all_gather | solution.py:453
  124.4 6.5 %fusion.66 = (f32[2,7,256]{2,1,0:T(8,128)S(1)}, f32[2,7,256,1024]{2,3,1,0:T(8,128)}) fusion(bf16[1024,2,64,1]{0,2,3,1:T(8,128)(2,1)S(1)} %bitcast.205, bf16[256,2,7,32]{0,3,2,1:T(8,128)(2,1)S(1)} %bitcast.209, bf16[256,2,7,32]{0,3,2,1:T(8,128)(2,1)S(1)} %bitcast.207, pred[256,1024]{0,1:T(8,128)(4,1)S(1)} %fusion.26), kind=kOutput, calls=%fused_computation.136 | convolution fusion | flops 481686016 | bytes 15677440 | tf_op jit(solution)/shard_map/qgjd,kgd->gjqk/dot_general | solution.py:57
  130.9 7.1 %fusion.3 = f32[2,7,256]{2,1,0:T(8,128)S(1)} fusion(f32[2,7,256,1024]{2,3,1,0:T(8,128)} %get-tuple-element.122, f32[2,7,256]{2,1,0:T(8,128)S(1)} %get-tuple-element.121), kind=kLoop, calls=%fused_computation.9 | loop fusion | flops 7336448 | bytes 14708736 | tf_op jit(solution)/shard_map/reduce_sum | solution.py:459
  138.1 6.6 %fusion.15 = bf16[2,64,7,256]{3,1,2,0:T(8,128)(2,1)S(1)} fusion(bf16[1024,2,64,1]{0,2,3,1:T(8,128)(2,1)S(1)} %bitcast.215, f32[2,7,256,1024]{2,3,1,0:T(8,128)} %get-tuple-element.122, f32[2,7,256]{2,1,0:T(8,128)S(1)} %fusion.3, f32[2,7,256]{2,1,0:T(8,128)S(1)} %get-tuple-element.121), kind=kOutput, calls=%fused_computation.33 | convolution fusion | flops 481001472 | bytes 15429632 | tf_op jit(solution)/shard_map/gjqk,kgd->qgjd/dot_general | solution.py:462
  148.8 7.2 %fusion.67 = f32[1024,1216]{0,1:T(8,128)} fusion(bf16[1024,896]{1,0:T(8,128)(2,1)} %bitcast.243, bf16[896,1216]{1,0:T(8,128)(2,1)} %bitcast.237), kind=kOutput, calls=%fused_computation.137 | convolution fusion | flops 2231369728 | bytes 8994816 | tf_op jit(solution)/shard_map/dot_general | solution.py:473
  156.0 32.8 %all-gather.2.cloned.1.call-done = bf16[1024,896]{1,0:T(8,128)(2,1)} async-done(((bf16[256,896]{1,0:T(8,128)(2,1)}), bf16[1024,896]{1,0:T(8,128)(2,1)}) %all-gather.2.cloned.1.call-update) | async-done | bytes 1835024 | tf_op jit(solution)/shard_map/all_gather | solution.py:470
  188.9 5.2 %fusion.68 = f32[1024,1216]{0,1:T(8,128)S(1)} fusion(bf16[1024,896]{1,0:T(8,128)(2,1)} %all-gather.2.cloned.1.call-done, bf16[896,1216]{1,0:T(8,128)(2,1)} %bitcast.241), kind=kOutput, calls=%fused_computation.138 | convolution fusion | flops 2231369728 | bytes 8994816 | tf_op jit(solution)/shard_map/dot_general | solution.py:471
  194.1 6.9 %multiply_convert_fusion = (bf16[1024,1216]{0,1:T(8,128)(2,1)}, bf16[1024,1216]{0,1:T(8,128)(2,1)S(1)}, bf16[1024,1216]{0,1:T(8,128)(2,1)}) fusion(f32[1024,1216]{0,1:T(8,128)S(1)} %fusion.68, f32[1024,1216]{0,1:T(8,128)S(1)} %copy-done.40, bf16[1024,896]{1,0:T(8,128)(2,1)S(1)} %copy-done.39, bf16[896,1216]{1,0:T(8,128)(2,1)S(1)} %bitcast.239), kind=kOutput, calls=%fused_computation.14 | convolution fusion | flops 2248802304 | bytes 21446656 | tf_op jit(solution)/shard_map/dot_general | solution.py:472
  209.5 5.0 %convolution_convert_fusion = bf16[896,1216]{0,1:T(8,128)(2,1)S(1)} fusion(bf16[1024,1216]{0,1:T(8,128)(2,1)} %get-tuple-element.82, bf16[1024,896]{1,0:T(8,128)(2,1)} %bitcast.244), kind=kOutput, calls=%fused_computation.21 | convolution fusion | flops 2232459264 | bytes 6504448 | tf_op jit(solution)/shard_map/dot_general | solution.py:20
  217.0 5.0 %convolution_convert_fusion.2 = bf16[896,1216]{0,1:T(8,128)(2,1)S(1)} fusion(bf16[1024,1216]{0,1:T(8,128)(2,1)} %copy-done.41, bf16[1024,896]{1,0:T(8,128)(2,1)} %all-gather.2.cloned.1.call-done), kind=kOutput, calls=%fused_computation.23 | convolution fusion | flops 2232459264 | bytes 6504448 | tf_op jit(solution)/shard_map/dot_general | solution.py:20
  224.6 5.0 %convolution_convert_fusion.1 = bf16[896,1216]{0,1:T(8,128)(2,1)S(1)} fusion(bf16[1024,1216]{0,1:T(8,128)(2,1)} %get-tuple-element.84, bf16[1024,896]{1,0:T(8,128)(2,1)} %all-gather.2.cloned.1.call-done), kind=kOutput, calls=%fused_computation.22 | convolution fusion | flops 2232459264 | bytes 6504448 | tf_op jit(solution)/shard_map/dot_general | solution.py:20
  232.3 6.7 %convolution_convert_fusion.4 = bf16[1024,896]{1,0:T(8,128)(2,1)} fusion(bf16[1024,1216]{0,1:T(8,128)(2,1)} %get-tuple-element.82, bf16[896,1216]{1,0:T(8,128)(2,1)} %bitcast.238), kind=kOutput, calls=%fused_computation.28 | convolution fusion | flops 2232287232 | bytes 6504448 | tf_op jit(solution)/shard_map/dot_general | solution.py:20
  239.0 7.6 %reduce-scatter.4.cloned.1.call-done = bf16[256,896]{1,0:T(8,128)(2,1)} async-done(((bf16[1024,896]{1,0:T(8,128)(2,1)}), bf16[256,896]{1,0:T(8,128)(2,1)}) %reduce-scatter.4.cloned.1.call-update) | async-done | bytes 458768 | tf_op jit(solution)/shard_map/reduce_scatter | solution.py:484
  254.5 7.7 %fusion.21 = bf16[2,64,1024]{2,1,0:T(8,128)(2,1)S(1)} fusion(bf16[256,2,7,64]{0,3,2,1:T(8,128)(2,1)S(1)} %bitcast.197, f32[2,7,256,1024]{2,3,1,0:T(8,128)} %get-tuple-element.122, f32[2,7,256]{2,1,0:T(8,128)S(1)} %copy-done.25), kind=kOutput, calls=%fused_computation.38 | convolution fusion | flops 477233152 | bytes 15415296 | tf_op jit(solution)/shard_map/gjqk,qgjd->kgd/dot_general | solution.py:516
  262.2 10.9 %fusion = (f32[2,7,256]{2,1,0:T(8,128)S(1)}, f32[2,1024,256,7]{2,1,3,0:T(8,128)}) fusion(f32[2,7,256,1024]{2,3,1,0:T(8,128)} %get-tuple-element.122, f32[2,7,256]{2,1,0:T(8,128)S(1)} %copy-done.25, bf16[1024,2,64,1]{0,2,3,1:T(8,128)(2,1)S(1)} %bitcast.216, bf16[256,2,7,64]{0,3,2,1:T(8,128)(2,1)S(1)} %bitcast.198), kind=kOutput, calls=%fused_computation.2 | convolution fusion | flops 480768512 | bytes 30109696 | tf_op jit(solution)/shard_map/qgjd,kgd->gjqk/dot_general | solution.py:515
  273.1 7.2 %fusion.2 = bf16[2,7,256,1024]{2,3,1,0:T(8,128)(2,1)S(1)} fusion(f32[2,1024,256,7]{2,1,3,0:T(8,128)} %get-tuple-element.126, f32[2,7,256,1024]{2,3,1,0:T(8,128)S(1)} %bitcast.186, f32[2,7,256]{2,1,0:T(8,128)S(1)} %get-tuple-element.125, f32[2,7,256]{2,1,0:T(8,128)S(1)} %copy-done.25), kind=kLoop, calls=%fused_computation.4 | loop fusion | flops 14680064 | bytes 36728832 | tf_op jit(solution)/shard_map/convert_element_type | solution.py:521
  290.7 14.4 %reduce-scatter.8.cloned.1.call-done = bf16[256,256]{0,1:T(8,128)(2,1)} async-done(((bf16[1024,256]{0,1:T(8,128)(2,1)}), bf16[256,256]{0,1:T(8,128)(2,1)}) %reduce-scatter.8.cloned.1.call-update) | async-done | bytes 131088 | tf_op jit(solution)/shard_map/reduce_scatter | solution.py:529
  312.3 5.4 %convolution_convert_fusion.3 = bf16[896,2048]{1,0:T(8,128)(2,1)} fusion(bf16[256,2048]{0,1:T(8,128)(2,1)} %bitcast.219, bf16[256,2048]{0,1:T(8,128)(2,1)} %bitcast.221, bf16[256,896]{1,0:T(8,128)(2,1)S(1)} %copy-done.24, bf16[256,896]{1,0:T(8,128)(2,1)S(1)} %get-tuple-element.95), kind=kOutput, calls=%fused_computation.24 | convolution fusion | flops 1886912512 | bytes 6684672 | tf_op jit(solution)/shard_map/dot_general | solution.py:20
  317.7 7.2 %reshape.338 = bf16[8,112,4,512]{3,2,1,0:T(4,128)(2,1)} reshape(bf16[896,2048]{1,0:T(8,128)(2,1)} %convolution_convert_fusion.3) | data formatting | bytes 7340032 | tf_op jit(solution)/shard_map/reshape | solution.py:551
  324.9 4.8 %copy.92 = bf16[8,112,4,512]{3,1,2,0:T(8,128)(2,1)} copy(bf16[8,112,4,512]{3,2,1,0:T(4,128)(2,1)} %reshape.338) | data formatting | bytes 7340032 | tf_op jit(solution)/shard_map/reshape | solution.py:551
  330.3 69.3 %shard_map.255 = (f32[112,512]{1,0:T(8,128)}, f32[112,1216]{1,0:T(8,128)}, f32[112,1216]{1,0:T(8,128)}, f32[112,1216]{1,0:T(8,128)}, f32[8,768]{1,0:T(8,128)}) custom-call(bf16[8,4,112,512]{3,2,1,0:T(8,128)(2,1)} %bitcast.193, bf16[8,112,1216]{2,1,0:T(8,128)(2,1)} %bitcast.195, bf16[8,112,1216]{2,1,0:T(8,128)(2,1)} %bitcast.196, ...), custom_call_target="tpu_custom_call" | custom-call | tf_op jit(solution)/shard_map/pallas_call | solution.py:323
  (204 shorter events, 81.1 us)
Async XLA Ops:
  7.2 181.7 %all-gather.2.cloned.1.call-start = ((), (), s32[]{:S(2)}) async-start(), calls=%async_computation.3 | async-start | bytes 2293760 | tf_op jit(solution)/shard_map/all_gather | solution.py:470
  86.0 14.0 %copy-start.32 = (f32[256]{0:T(256)}, f32[256]{0:T(256)S(1)}, u32[]{:S(2)}) copy-start(f32[256]{0:T(256)S(1)} %get-tuple-element.118) | copy-start | bytes 3076
  104.9 43.0 %copy-start.26 = (f32[896]{0:T(1024)}, f32[896]{0:T(1024)S(1)}, u32[]{:S(2)}) copy-start(f32[896]{0:T(1024)S(1)} %reshape.347) | copy-start | bytes 10756
  106.9 24.0 %copy-start.17 = (f32[256,32]{0,1:T(8,128)}, f32[256,32]{0,1:T(8,128)S(1)}, u32[]{:S(2)}) copy-start(f32[256,32]{0,1:T(8,128)S(1)} %get-tuple-element.115) | copy-start | bytes 98308
  107.0 23.9 %copy-start.19 = (f32[256,32]{0,1:T(8,128)}, f32[256,32]{0,1:T(8,128)S(1)}, u32[]{:S(2)}) copy-start(f32[256,32]{0,1:T(8,128)S(1)} %get-tuple-element.116) | copy-start | bytes 98308
  107.4 23.5 %copy-start.7 = (bf16[256,14,32]{0,2,1:T(8,128)(2,1)}, bf16[256,14,32]{0,2,1:T(8,128)(2,1)S(1)}, u32[]{:S(2)}) copy-start(bf16[256,14,32]{0,2,1:T(8,128)(2,1)S(1)} %get-tuple-element.91) | copy-start | bytes 688132
  107.4 23.5 %copy-start.9 = (bf16[256,14,32]{0,2,1:T(8,128)(2,1)}, bf16[256,14,32]{0,2,1:T(8,128)(2,1)S(1)}, u32[]{:S(2)}) copy-start(bf16[256,14,32]{0,2,1:T(8,128)(2,1)S(1)} %get-tuple-element.92) | copy-start | bytes 688132
  124.1 13.9 %copy-start.13 = (bf16[1024,128]{0,1:T(8,128)(2,1)}, bf16[1024,128]{0,1:T(8,128)(2,1)S(1)}, u32[]{:S(2)}) copy-start(bf16[1024,128]{0,1:T(8,128)(2,1)S(1)} %get-tuple-element.94) | copy-start | bytes 786436
  148.8 97.8 %reduce-scatter.4.cloned.1.call-start = ((), (), s32[]{:S(2)}) async-start(), calls=%async_computation.4 | async-start | bytes 2293760 | tf_op jit(solution)/shard_map/reduce_scatter | solution.py:484
  208.2 96.9 %reduce-scatter.8.cloned.1.call-start = ((), (), s32[]{:S(2)}) async-start(), calls=%async_computation.6 | async-start | bytes 655360 | tf_op jit(solution)/shard_map/reduce_scatter | solution.py:529
  232.3 14.3 %copy-start.27 = (f32[896]{0:T(1024)S(1)}, f32[896]{0:T(1024)}, u32[]{:S(2)}) copy-start(f32[896]{0:T(1024)} %copy-done.26) | copy-start | bytes 10756
  232.3 14.3 %copy-start.31 = (f32[256]{0:T(256)S(1)}, f32[256]{0:T(256)}, u32[]{:S(2)}) copy-start(f32[256]{0:T(256)} %copy-done.30) | copy-start | bytes 3076
  232.3 15.7 %copy-start.2 = (bf16[1,256,896]{2,1,0:T(8,128)(2,1)S(1)}, bf16[1,256,896]{2,1,0:T(8,128)(2,1)}, u32[]{:S(2)}) copy-start(bf16[1,256,896]{2,1,0:T(8,128)(2,1)} %param.17) | copy-start | bytes 1376260
  232.3 15.7 %copy-start.34 = (f32[256]{0:T(256)S(1)}, f32[256]{0:T(256)}, u32[]{:S(2)}) copy-start(f32[256]{0:T(256)} %get-tuple-element.119) | copy-start | bytes 3076
  254.5 18.6 %slice-start = ((s8[14680064]{0:T(1024)(128)(4,1)}), s8[4194304]{0:T(1024)(128)(4,1)S(1)}, s32[]{:S(2)}) async-start(s8[14680064]{0:T(1024)(128)(4,1)} %bitcast.185), calls=%async_computation.7 | async-start | bytes 8388608
  254.5 18.6 %slice-start.1 = ((s8[14680064]{0:T(1024)(128)(4,1)}), s8[4194304]{0:T(1024)(128)(4,1)S(1)}, s32[]{:S(2)}) async-start(s8[14680064]{0:T(1024)(128)(4,1)} %bitcast.185), calls=%async_computation.8 | async-start | bytes 8388608
  262.2 10.9 %slice-start.2 = ((s8[14680064]{0:T(1024)(128)(4,1)}), s8[4194304]{0:T(1024)(128)(4,1)S(1)}, s32[]{:S(2)}) async-start(s8[14680064]{0:T(1024)(128)(4,1)} %bitcast.185), calls=%async_computation.9 | async-start | bytes 8388608
  262.2 10.9 %slice-start.3 = ((s8[14680064]{0:T(1024)(128)(4,1)}), s8[2097152]{0:T(1024)(128)(4,1)S(1)}, s32[]{:S(2)}) async-start(s8[14680064]{0:T(1024)(128)(4,1)} %bitcast.185), calls=%async_computation.10 | async-start | bytes 4194304
  284.1 122.4 %reduce-scatter.6.cloned.1.call-start = ((), (), s32[]{:S(2)}) async-start(), calls=%async_computation.5 | async-start | bytes 2293760 | tf_op jit(solution)/shard_map/reduce_scatter | solution.py:495
  290.2 17.0 %copy-start.29 = (f32[896]{0:T(1024)S(1)}, f32[896]{0:T(1024)}, u32[]{:S(2)}) copy-start(f32[896]{0:T(1024)} %copy-done.28) | copy-start | bytes 10756
  290.2 17.0 %copy-start.33 = (f32[256]{0:T(256)S(1)}, f32[256]{0:T(256)}, u32[]{:S(2)}) copy-start(f32[256]{0:T(256)} %copy-done.32) | copy-start | bytes 3076
  330.3 76.2 %copy-start.3 = (bf16[256,896]{1,0:T(8,128)(2,1)S(1)}, bf16[256,896]{1,0:T(8,128)(2,1)}, u32[]{:S(2)}) copy-start(bf16[256,896]{1,0:T(8,128)(2,1)} %reduce-scatter.4.cloned.1.call-done) | copy-start | bytes 1376260
  330.3 76.2 %copy-start.36 = (f32[256]{0:T(256)S(1)}, f32[256]{0:T(256)}, u32[]{:S(2)}) copy-start(f32[256]{0:T(256)} %get-tuple-element.117) | copy-start | bytes 3076
  399.7 10.7 %copy-start.22 = (f32[112,1216]{1,0:T(8,128)S(1)}, f32[112,1216]{1,0:T(8,128)}, u32[]{:S(2)}) copy-start(f32[112,1216]{1,0:T(8,128)} %get-tuple-element.154) | copy-start | bytes 1634308
  (27 other events, 130.6 us)
Sparse Core Ops, SparseCore 0:
  148.9 39.9 all-gather.1
  208.3 38.2 reduce-scatter.3
  284.2 20.7 reduce-scatter.7
  307.2 39.1 reduce-scatter.5
